TPU v7x, 32 devices: a whole 2x2x4 slice. The times are simulated.
32 devices in a mesh: dp: 2 (over core), ctx: 8 (over z, y), fsdp: 2 (over x).
Axes of the slice: x: 2, y: 2, z: 4, core: 2. Of those that a mesh axis runs over, the one named last changes fastest.
Arguments:
- tokens: bfloat16 [4, 1536, 1024], P(('dp', 'fsdp'), 'ctx'), may hold values from -6 to 6
- attn_gain: bfloat16 [1024], P('fsdp'), may hold values from 0.099609375 to 1.8984375
- qkv_weight: bfloat16 [1024, 3072], P('fsdp'), may hold values from -0.21875 to 0.21875
- out_weight: bfloat16 [1024, 1024], P('fsdp'), may hold values from -3 to 3
- mlp_gain: bfloat16 [1024], P('fsdp'), may hold values from 0.099609375 to 1.8984375
- in_weight: bfloat16 [1024, 5248], P('fsdp'), may hold values from -0.1875 to 0.1875
- down_weight: bfloat16 [2624, 1024], P('fsdp'), may hold values from -0.125 to 0.125
- cotangent: bfloat16 [4, 1536, 1024], P(('dp', 'fsdp'), 'ctx'), may hold values from -6 to 6
Outputs:
- output: bfloat16 [4, 1536, 1024], P(('dp', 'fsdp'), 'ctx')
- grad_tokens: float32 [4, 1536, 1024], P(('dp', 'fsdp'), 'ctx')
- grad_attn_gain: float32 [1024], P('fsdp')
- grad_qkv_weight: float32 [1024, 3072], P('fsdp')
- grad_out_weight: float32 [1024, 1024], P('fsdp')
- grad_mlp_gain: float32 [1024], P('fsdp')
- grad_in_weight: float32 [1024, 5248], P('fsdp')
- grad_down_weight: float32 [2624, 1024], P('fsdp')
All inputs are finite; a program needn't handle non-finite values.
Results may differ from a plain program's by a relative error of at most 0.02.
Values may be sent and summed in bfloat16 or wider, within the bound.
A program may use at most 192 MiB of HBM per device.

v0:
```python
import jax
import jax.numpy as jnp
from jax import lax
from jax.sharding import PartitionSpec as P

HEAD_DIM = 64


theta_base = 160000.0
epsilon = 1e-05


def from_behind(value, axis, steps):
    count = lax.axis_size(axis)
    pairs = [(source, (source + steps) % count) for source in range(count)]
    return lax.ppermute(value, axis, pairs)


def layer_norm(values, gain):
    centred = values - jnp.mean(values, -1, keepdims=True)
    spread = jnp.mean(centred * centred, -1, keepdims=True)
    return centred * lax.rsqrt(spread + epsilon) * gain


def rope_tables(positions, head_size):
    middle = head_size // 2
    inverse = theta_base ** (-(jnp.arange(middle).astype(jnp.float32) * 2.0) / head_size)
    angles = positions[:, None] * inverse[None, :]
    cosine = jnp.cos(angles)
    sine = jnp.sin(angles)
    return (jnp.concatenate([cosine, cosine], -1), jnp.concatenate([sine, sine], -1))


def rotate(values, cosine, sine):
    middle = values.shape[-1] // 2
    turned = jnp.concatenate([-values[..., middle:], values[..., :middle]], -1)
    return values * cosine[:, None, :] + turned * sine[:, None, :]


def unrotate(grads_in, cosine, sine):
    middle = grads_in.shape[-1] // 2
    scaled = grads_in * sine[:, None, :]
    return grads_in * cosine[:, None, :] + jnp.concatenate(
        [scaled[..., middle:], -scaled[..., :middle]], -1
    )


def geglu(expanded):
    middle = expanded.shape[-1] // 2
    return jax.nn.gelu(expanded[:, :middle], approximate=False) * expanded[:, middle:]


def turn_keys(paired):
    return from_behind(paired, "ctx", 1)


def turn_back_keys(paired):
    return from_behind(paired, "ctx", 1)


def turn_grads(grad_pair):
    return from_behind(grad_pair.astype(jnp.bfloat16), "ctx", 1).astype(grad_pair.dtype)


def attend_block(queries, paired, state, scale):
    best, total, summed = state
    scores = (
        jnp.einsum("qhe,khe->hqk", queries, paired[0], preferred_element_type=jnp.float32) * scale
    )
    peak = jnp.maximum(best, jnp.max(scores, -1))
    shrink = jnp.exp(best - peak)
    weights = jnp.exp(scores - peak[..., None])
    total = total * shrink + jnp.sum(weights, -1)
    update = jnp.einsum(
        "hqk,khe->qhe", weights.astype(jnp.bfloat16), paired[1], preferred_element_type=jnp.float32
    )
    summed = summed * jnp.transpose(shrink)[:, :, None] + update
    return (peak, total, summed)


def back_block(queries, grad_attended, log_total, delta, paired, grad_pair, grad_queries, scale):
    scores = (
        jnp.einsum("qhe,khe->hqk", queries, paired[0], preferred_element_type=jnp.float32) * scale
    )
    probs = jnp.exp(scores - log_total[..., None])
    grad_probs = jnp.einsum(
        "qhe,khe->hqk", grad_attended, paired[1], preferred_element_type=jnp.float32
    )
    grad_scores = (probs * (grad_probs - delta[..., None])).astype(jnp.bfloat16)
    grad_values = jnp.einsum(
        "hqk,qhe->khe",
        probs.astype(jnp.bfloat16),
        grad_attended,
        preferred_element_type=jnp.float32,
    )
    grad_keys = (
        jnp.einsum("hqk,qhe->khe", grad_scores, queries, preferred_element_type=jnp.float32) * scale
    )
    grad_queries = (
        grad_queries
        + jnp.einsum("hqk,khe->qhe", grad_scores, paired[0], preferred_element_type=jnp.float32)
        * scale
    )
    grad_pair = grad_pair + jnp.stack([grad_keys, grad_values])
    return (grad_pair, grad_queries)


def local(tokens, attn_gain, qkv_weight, out_weight, mlp_gain, in_weight, down_weight, cotangent):
    row_count = tokens.shape[1]
    cycle_size = lax.axis_size("ctx")
    gain_one, w_qkv, w_out = (
        lax.all_gather(attn_gain, "fsdp", axis=0, tiled=True),
        lax.all_gather(qkv_weight, "fsdp", axis=0, tiled=True),
        lax.all_gather(out_weight, "fsdp", axis=0, tiled=True),
    )
    width = w_out.shape[1]
    head_size = HEAD_DIM
    heads = width // head_size
    shaped = (row_count, heads, head_size)
    scale = head_size ** (-0.5)
    inputs = tokens[0].astype(jnp.float32)
    positions = (lax.axis_index("ctx") * row_count + jnp.arange(row_count, dtype=jnp.int32)).astype(
        jnp.float32
    )
    cosine, sine = rope_tables(positions, head_size)
    gain_att = gain_one.astype(jnp.float32)
    normed = layer_norm(inputs, gain_att).astype(jnp.bfloat16)
    projected = jnp.dot(normed, w_qkv, preferred_element_type=jnp.float32)
    queries = rotate(projected[:, :width].reshape(shaped), cosine, sine).astype(jnp.bfloat16)
    keys = rotate(projected[:, width : 2 * width].reshape(shaped), cosine, sine).astype(
        jnp.bfloat16
    )
    values = projected[:, 2 * width :].reshape(shaped).astype(jnp.bfloat16)
    local_pair = jnp.stack([keys, values])
    start_state = (
        jnp.full((heads, row_count), -1e30, jnp.float32),
        jnp.zeros((heads, row_count), jnp.float32),
        jnp.zeros(shaped, jnp.float32),
    )

    def forward_turn(number, carry):
        state, paired = carry
        return (attend_block(queries, paired, state, scale), turn_keys(paired))

    state, paired = lax.fori_loop(0, cycle_size - 1, forward_turn, (start_state, local_pair))
    best, total, summed = attend_block(queries, paired, state, scale)
    attended = summed / jnp.transpose(total)[:, :, None]
    log_total = best + jnp.log(total)
    attended_low = attended.reshape(row_count, width).astype(jnp.bfloat16)
    residual = inputs + jnp.dot(attended_low, w_out, preferred_element_type=jnp.float32)
    gain_two, w_in, w_down = (
        lax.all_gather(mlp_gain, "fsdp", axis=0, tiled=True),
        lax.all_gather(in_weight, "fsdp", axis=0, tiled=True),
        lax.all_gather(down_weight, "fsdp", axis=0, tiled=True),
    )
    gain_mlp = gain_two.astype(jnp.float32)
    normed_mlp = layer_norm(residual, gain_mlp).astype(jnp.bfloat16)
    expanded = jnp.dot(normed_mlp, w_in, preferred_element_type=jnp.float32)
    gated = geglu(expanded).astype(jnp.bfloat16)
    output = residual + jnp.dot(gated, w_down, preferred_element_type=jnp.float32)
    grad_output = cotangent[0]
    grad_down = jnp.einsum("tf,td->fd", gated, grad_output, preferred_element_type=jnp.float32)
    grad_gated = jnp.einsum("td,fd->tf", grad_output, w_down, preferred_element_type=jnp.float32)
    unused_gate, pull_gate = jax.vjp(geglu, expanded)
    grad_expanded = pull_gate(grad_gated)[0].astype(jnp.bfloat16)
    grad_in = jnp.einsum("tf,tg->fg", normed_mlp, grad_expanded, preferred_element_type=jnp.float32)
    grad_normed_mlp = jnp.einsum(
        "tg,fg->tf", grad_expanded, w_in, preferred_element_type=jnp.float32
    )
    unused_mlp, pull_mlp = jax.vjp(layer_norm, residual, gain_mlp)
    grad_residual_mlp, grad_gain_mlp = pull_mlp(grad_normed_mlp)
    grad_residual = grad_output.astype(jnp.float32) + grad_residual_mlp
    grad_branch = grad_residual.astype(jnp.bfloat16)
    grad_wout = jnp.einsum(
        "tf,td->fd", attended_low, grad_branch, preferred_element_type=jnp.float32
    )
    grad_attended = (
        jnp.einsum("td,fd->tf", grad_branch, w_out, preferred_element_type=jnp.float32)
        .astype(jnp.bfloat16)
        .reshape(shaped)
    )
    delta = jnp.einsum("qhe,qhe->hq", grad_attended.astype(jnp.float32), attended)

    def backward_turn(number, carry):
        paired_now, grad_pair, grad_queries = carry
        grad_pair, grad_queries = back_block(
            queries, grad_attended, log_total, delta, paired_now, grad_pair, grad_queries, scale
        )
        return (turn_back_keys(paired_now), turn_grads(grad_pair), grad_queries)

    start_back = (local_pair, jnp.zeros((2,) + shaped, jnp.float32), jnp.zeros(shaped, jnp.float32))
    paired_now, grad_pair, grad_queries = lax.fori_loop(
        0, cycle_size - 1, backward_turn, start_back
    )
    grad_pair, grad_queries = back_block(
        queries, grad_attended, log_total, delta, paired_now, grad_pair, grad_queries, scale
    )
    grad_pair = turn_grads(grad_pair)
    grad_projected = jnp.concatenate(
        [
            unrotate(grad_queries, cosine, sine).reshape(row_count, width),
            unrotate(grad_pair[0], cosine, sine).reshape(row_count, width),
            grad_pair[1].reshape(row_count, width),
        ],
        1,
    ).astype(jnp.bfloat16)
    grad_wqkv = jnp.einsum("tf,tg->fg", normed, grad_projected, preferred_element_type=jnp.float32)
    grad_normed = jnp.einsum("tg,fg->tf", grad_projected, w_qkv, preferred_element_type=jnp.float32)
    unused_att, pull_att = jax.vjp(layer_norm, inputs, gain_att)
    grad_inputs_att, grad_gain_att = pull_att(grad_normed)
    grad_inputs = grad_residual + grad_inputs_att
    halves = (
        lax.psum_scatter(
            grad_wqkv.astype(jnp.bfloat16), "fsdp", scatter_dimension=0, tiled=True
        ).astype(jnp.float32),
        lax.psum_scatter(
            grad_wout.astype(jnp.bfloat16), "fsdp", scatter_dimension=0, tiled=True
        ).astype(jnp.float32),
        lax.psum_scatter(
            grad_in.astype(jnp.bfloat16), "fsdp", scatter_dimension=0, tiled=True
        ).astype(jnp.float32),
        lax.psum_scatter(
            grad_down.astype(jnp.bfloat16), "fsdp", scatter_dimension=0, tiled=True
        ).astype(jnp.float32),
        lax.psum_scatter(
            grad_gain_att.astype(jnp.bfloat16), "fsdp", scatter_dimension=0, tiled=True
        ).astype(jnp.float32),
        lax.psum_scatter(
            grad_gain_mlp.astype(jnp.bfloat16), "fsdp", scatter_dimension=0, tiled=True
        ).astype(jnp.float32),
    )
    pieces = (
        lax.psum_scatter(halves[0], ("dp", "ctx"), scatter_dimension=1, tiled=True),
        lax.psum_scatter(halves[1], ("dp", "ctx"), scatter_dimension=1, tiled=True),
        lax.psum_scatter(halves[2], ("dp", "ctx"), scatter_dimension=1, tiled=True),
        lax.psum_scatter(halves[3], ("dp", "ctx"), scatter_dimension=1, tiled=True),
        lax.psum_scatter(halves[4][None, :], ("dp", "ctx"), scatter_dimension=1, tiled=True),
        lax.psum_scatter(halves[5][None, :], ("dp", "ctx"), scatter_dimension=1, tiled=True),
    )
    summed_grads = (
        lax.all_gather(pieces[0].astype(jnp.bfloat16), ("dp", "ctx"), axis=1, tiled=True).astype(
            jnp.float32
        ),
        lax.all_gather(pieces[1].astype(jnp.bfloat16), ("dp", "ctx"), axis=1, tiled=True).astype(
            jnp.float32
        ),
        lax.all_gather(pieces[2].astype(jnp.bfloat16), ("dp", "ctx"), axis=1, tiled=True).astype(
            jnp.float32
        ),
        lax.all_gather(pieces[3].astype(jnp.bfloat16), ("dp", "ctx"), axis=1, tiled=True).astype(
            jnp.float32
        ),
        lax.all_gather(pieces[4].astype(jnp.bfloat16), ("dp", "ctx"), axis=1, tiled=True).astype(
            jnp.float32
        ),
        lax.all_gather(pieces[5].astype(jnp.bfloat16), ("dp", "ctx"), axis=1, tiled=True).astype(
            jnp.float32
        ),
    )
    return (
        output.astype(jnp.bfloat16)[None],
        grad_inputs[None],
        summed_grads[4][0],
        summed_grads[0],
        summed_grads[1],
        summed_grads[5][0],
        summed_grads[2],
        summed_grads[3],
    )


def solution(mesh):
    in_specs = (
        P(("dp", "fsdp"), "ctx", None),
        P("fsdp"),
        P("fsdp", None),
        P("fsdp", None),
        P("fsdp"),
        P("fsdp", None),
        P("fsdp", None),
        P(("dp", "fsdp"), "ctx", None),
    )
    out_specs = (
        P(("dp", "fsdp"), "ctx", None),
        P(("dp", "fsdp"), "ctx", None),
        P("fsdp"),
        P("fsdp", None),
        P("fsdp", None),
        P("fsdp"),
        P("fsdp", None),
        P("fsdp", None),
    )
    return jax.shard_map(local, mesh=mesh, in_specs=in_specs, out_specs=out_specs, check_vma=False)
```

profile of v0, /device:TPU:0, one launch (start us, length us, event | category | flops | bytes accessed | tf_op | source)
XLA Modules:
  0.0 1709.3 jit_solution(5507346467267870675)
XLA Ops:
  22.2 70.4 %all-gather.11.cloned.1.call-done = bf16[1024,3072]{1,0:T(8,128)(2,1)} async-done(((bf16[512,3072]{1,0:T(8,128)(2,1)}), bf16[1024,3072]{1,0:T(8,128)(2,1)}) %all-gather.11.cloned.1.call-update) | async-done | bytes 6291472 | tf_op jit(solution)/shard_map/all_gather | solution.py:113
  103.9 192.0 %while.32 = (s32[]{:T(128)}, f32[16,192]{1,0:T(8,128)S(1)}, f32[16,192]{1,0:T(8,128)}, f32[192,16,64]{0,2,1:T(8,128)}, bf16[2,192,16,64]{1,3,2,0:T(8,128)(2,1)},...) while((s32[]{:T(128)}, f32[16,192]{1,0:T(8,128)S(1)}, f32[16,192]{1,0:T(8,128)}, ...), condition=%wide.region_5.0_spmd.clone, body=%wide.region_2.0_spmd.clone.sunk | while | flops 156321792 | bytes 21528832 | solution.py:145
  114.0 20.6 %collective-permute-done = bf16[2,192,16,64]{1,3,2,0:T(8,128)(2,1)} collective-permute-done((bf16[2,192,16,64]{1,3,2,0:T(8,128)(2,1)}, bf16[2,192,16,64]{1,3,2,0:T(8,128)(2,1)}, u32[]{:S(2)}, u32[]{:S(2)}) %collective-permute-start) | collective-permute-done | bytes 786464 | tf_op jit(solution)/shard_map/while/body/eval_jaxpr/ppermute | solution.py:16
  143.3 20.6 %collective-permute-done = bf16[2,192,16,64]{1,3,2,0:T(8,128)(2,1)} collective-permute-done((bf16[2,192,16,64]{1,3,2,0:T(8,128)(2,1)}, bf16[2,192,16,64]{1,3,2,0:T(8,128)(2,1)}, u32[]{:S(2)}, u32[]{:S(2)}) %collective-permute-start) | collective-permute-done | bytes 786464 | tf_op jit(solution)/shard_map/while/body/eval_jaxpr/ppermute | solution.py:16
  172.1 20.1 %collective-permute-done = bf16[2,192,16,64]{1,3,2,0:T(8,128)(2,1)} collective-permute-done((bf16[2,192,16,64]{1,3,2,0:T(8,128)(2,1)}, bf16[2,192,16,64]{1,3,2,0:T(8,128)(2,1)}, u32[]{:S(2)}, u32[]{:S(2)}) %collective-permute-start) | collective-permute-done | bytes 786464 | tf_op jit(solution)/shard_map/while/body/eval_jaxpr/ppermute | solution.py:16
  200.3 19.2 %collective-permute-done = bf16[2,192,16,64]{1,3,2,0:T(8,128)(2,1)} collective-permute-done((bf16[2,192,16,64]{1,3,2,0:T(8,128)(2,1)}, bf16[2,192,16,64]{1,3,2,0:T(8,128)(2,1)}, u32[]{:S(2)}, u32[]{:S(2)}) %collective-permute-start) | collective-permute-done | bytes 786464 | tf_op jit(solution)/shard_map/while/body/eval_jaxpr/ppermute | solution.py:16
  227.6 18.3 %collective-permute-done = bf16[2,192,16,64]{1,3,2,0:T(8,128)(2,1)} collective-permute-done((bf16[2,192,16,64]{1,3,2,0:T(8,128)(2,1)}, bf16[2,192,16,64]{1,3,2,0:T(8,128)(2,1)}, u32[]{:S(2)}, u32[]{:S(2)}) %collective-permute-start) | collective-permute-done | bytes 786464 | tf_op jit(solution)/shard_map/while/body/eval_jaxpr/ppermute | solution.py:16
  254.0 17.3 %collective-permute-done = bf16[2,192,16,64]{1,3,2,0:T(8,128)(2,1)} collective-permute-done((bf16[2,192,16,64]{1,3,2,0:T(8,128)(2,1)}, bf16[2,192,16,64]{1,3,2,0:T(8,128)(2,1)}, u32[]{:S(2)}, u32[]{:S(2)}) %collective-permute-start) | collective-permute-done | bytes 786464 | tf_op jit(solution)/shard_map/while/body/eval_jaxpr/ppermute | solution.py:16
  313.1 19.7 %all-gather.17.cloned.1.call-done = bf16[2624,1024]{1,0:T(8,128)(2,1)} async-done(((bf16[1312,1024]{1,0:T(8,128)(2,1)}), bf16[2624,1024]{1,0:T(8,128)(2,1)}) %all-gather.17.cloned.1.call-update) | async-done | bytes 5373968 | tf_op jit(solution)/shard_map/all_gather | solution.py:154
  370.2 411.6 %while.33 = (s32[]{:T(128)}, bf16[2,192,16,64]{1,3,2,0:T(8,128)(2,1)}, f32[2,192,16,64]{1,3,2,0:T(8,128)}, f32[192,16,64]{0,2,1:T(8,128)}, bf16[192,16,64]{0,2,1...) while((s32[]{:T(128)}, ...), condition=%wide.region_13.0_spmd.clone, body=%wide.region_12.0_spmd.clone.sunk | while | flops 384958464 | bytes 35614992 | solution.py:192
  385.5 24.5 %collective-permute-done.2 = bf16[2,192,16,64]{1,3,2,0:T(8,128)(2,1)} collective-permute-done((bf16[2,192,16,64]{1,3,2,0:T(8,128)(2,1)}, bf16[2,192,16,64]{1,3,2,0:T(8,128)(2,1)}, u32[]{:S(2)}, u32[]{:S(2)}) %collective-permute-start.2) | collective-permute-done | bytes 786464 | tf_op jit(solution)/shard_map/while/body/eval_jaxpr/ppermute | solution.py:16
  412.9 18.4 %collective-permute-done.1 = bf16[2,192,16,64]{1,3,2,0:T(8,128)(2,1)} collective-permute-done((bf16[2,192,16,64]{1,3,2,0:T(8,128)(2,1)S(1)}, bf16[2,192,16,64]{1,3,2,0:T(8,128)(2,1)}, u32[]{:S(2)}, u32[]{:S(2)}) %collective-permute-start.1) | collective-permute-done | bytes 786464 | tf_op jit(solution)/shard_map/while/body/eval_jaxpr/ppermute | solution.py:16
  446.5 25.3 %collective-permute-done.2 = bf16[2,192,16,64]{1,3,2,0:T(8,128)(2,1)} collective-permute-done((bf16[2,192,16,64]{1,3,2,0:T(8,128)(2,1)}, bf16[2,192,16,64]{1,3,2,0:T(8,128)(2,1)}, u32[]{:S(2)}, u32[]{:S(2)}) %collective-permute-start.2) | collective-permute-done | bytes 786464 | tf_op jit(solution)/shard_map/while/body/eval_jaxpr/ppermute | solution.py:16
  474.6 17.5 %collective-permute-done.1 = bf16[2,192,16,64]{1,3,2,0:T(8,128)(2,1)} collective-permute-done((bf16[2,192,16,64]{1,3,2,0:T(8,128)(2,1)S(1)}, bf16[2,192,16,64]{1,3,2,0:T(8,128)(2,1)}, u32[]{:S(2)}, u32[]{:S(2)}) %collective-permute-start.1) | collective-permute-done | bytes 786464 | tf_op jit(solution)/shard_map/while/body/eval_jaxpr/ppermute | solution.py:16
  506.3 26.3 %collective-permute-done.2 = bf16[2,192,16,64]{1,3,2,0:T(8,128)(2,1)} collective-permute-done((bf16[2,192,16,64]{1,3,2,0:T(8,128)(2,1)}, bf16[2,192,16,64]{1,3,2,0:T(8,128)(2,1)}, u32[]{:S(2)}, u32[]{:S(2)}) %collective-permute-start.2) | collective-permute-done | bytes 786464 | tf_op jit(solution)/shard_map/while/body/eval_jaxpr/ppermute | solution.py:16
  566.0 26.3 %collective-permute-done.2 = bf16[2,192,16,64]{1,3,2,0:T(8,128)(2,1)} collective-permute-done((bf16[2,192,16,64]{1,3,2,0:T(8,128)(2,1)}, bf16[2,192,16,64]{1,3,2,0:T(8,128)(2,1)}, u32[]{:S(2)}, u32[]{:S(2)}) %collective-permute-start.2) | collective-permute-done | bytes 786464 | tf_op jit(solution)/shard_map/while/body/eval_jaxpr/ppermute | solution.py:16
  624.9 26.3 %collective-permute-done.2 = bf16[2,192,16,64]{1,3,2,0:T(8,128)(2,1)} collective-permute-done((bf16[2,192,16,64]{1,3,2,0:T(8,128)(2,1)}, bf16[2,192,16,64]{1,3,2,0:T(8,128)(2,1)}, u32[]{:S(2)}, u32[]{:S(2)}) %collective-permute-start.2) | collective-permute-done | bytes 786464 | tf_op jit(solution)/shard_map/while/body/eval_jaxpr/ppermute | solution.py:16
  682.8 26.3 %collective-permute-done.2 = bf16[2,192,16,64]{1,3,2,0:T(8,128)(2,1)} collective-permute-done((bf16[2,192,16,64]{1,3,2,0:T(8,128)(2,1)}, bf16[2,192,16,64]{1,3,2,0:T(8,128)(2,1)}, u32[]{:S(2)}, u32[]{:S(2)}) %collective-permute-start.2) | collective-permute-done | bytes 786464 | tf_op jit(solution)/shard_map/while/body/eval_jaxpr/ppermute | solution.py:16
  739.8 26.3 %collective-permute-done.2 = bf16[2,192,16,64]{1,3,2,0:T(8,128)(2,1)} collective-permute-done((bf16[2,192,16,64]{1,3,2,0:T(8,128)(2,1)}, bf16[2,192,16,64]{1,3,2,0:T(8,128)(2,1)}, u32[]{:S(2)}, u32[]{:S(2)}) %collective-permute-start.2) | collective-permute-done | bytes 786464 | tf_op jit(solution)/shard_map/while/body/eval_jaxpr/ppermute | solution.py:16
  788.3 21.1 %collective-permute-done.3 = bf16[2,192,16,64]{1,3,2,0:T(8,128)(2,1)S(1)} collective-permute-done((bf16[2,192,16,64]{1,3,2,0:T(8,128)(2,1)S(1)}, bf16[2,192,16,64]{1,3,2,0:T(8,128)(2,1)S(1)}, u32[]{:S(2)}, u32[]{:S(2)}) %collective-permute-start.3) | collective-permute-done | bytes 786464 | tf_op jit(solution)/shard_map/ppermute | solution.py:16
  835.9 56.9 %reduce-scatter.23.cloned.1.call-done = bf16[512,3072]{1,0:T(8,128)(2,1)} async-done(((bf16[1024,3072]{1,0:T(8,128)(2,1)}), bf16[512,3072]{1,0:T(8,128)(2,1)}) %reduce-scatter.23.cloned.1.call-update) | async-done | bytes 3145744 | tf_op jit(solution)/shard_map/reduce_scatter | solution.py:213
  898.3 122.3 %reduce-scatter.27.cloned.1.call-done = bf16[512,5248]{1,0:T(8,128)(2,1)} async-done(((bf16[1024,5248]{1,0:T(8,128)(2,1)}), bf16[512,5248]{1,0:T(8,128)(2,1)}) %reduce-scatter.27.cloned.1.call-update) | async-done | bytes 5373968 | tf_op jit(solution)/shard_map/reduce_scatter | solution.py:219
  1043.7 43.4 %reduce-scatter.35.cloned.1.call-done = f32[64,512]{1,0:T(8,128)} async-done(((f32[1024,512]{1,0:T(8,128)}), f32[64,512]{1,0:T(8,128)}) %reduce-scatter.35.cloned.1.call-update) | async-done | bytes 131088
  1088.6 82.7 %reduce-scatter.41.cloned.1.call-done = f32[64,1312]{1,0:T(8,128)} async-done(((f32[1024,1312]{1,0:T(8,128)}), f32[64,1312]{1,0:T(8,128)}) %reduce-scatter.41.cloned.1.call-update) | async-done | bytes 335888
  1173.1 87.2 %reduce-scatter.33.cloned.1.call-done = f32[192,512]{1,0:T(8,128)} async-done(((f32[3072,512]{1,0:T(8,128)}), f32[192,512]{1,0:T(8,128)}) %reduce-scatter.33.cloned.1.call-update) | async-done | bytes 393232
  1262.0 123.4 %reduce-scatter.39.cloned.1.call-done = f32[328,512]{1,0:T(8,128)} async-done(((f32[5248,512]{1,0:T(8,128)}), f32[328,512]{1,0:T(8,128)}) %reduce-scatter.39.cloned.1.call-update) | async-done | bytes 671760
  1394.6 50.4 %reduce-scatter.31.cloned.1.call-done = f32[32,1]{1,0:T(8,128)} async-done(((f32[512,1]{1,0:T(8,128)}), f32[32,1]{1,0:T(8,128)}) %reduce-scatter.31.cloned.1.call-update) | async-done | bytes 144
  1445.8 57.4 %reduce-scatter.37.cloned.1.call-done = f32[32,1]{1,0:T(8,128)} async-done(((f32[512,1]{1,0:T(8,128)}), f32[32,1]{1,0:T(8,128)}) %reduce-scatter.37.cloned.1.call-update) | async-done | bytes 144
  1504.4 31.1 %all-reduce.6 = (bf16[512]{0:T(512)(128)(2,1)S(1)}, bf16[512]{0:T(512)(128)(2,1)S(1)}) all-reduce(bf16[512]{0:T(512)(128)(2,1)S(1)} %dynamic-update-slice, bf16[512]{0:T(512)(128)(2,1)S(1)} %dynamic-update-slice.1), channel_id=1, replica_groups=mesh['dp'=2,'ctx'=8,'fsdp'=2] {'dp','ctx'}, use_global_device_ids=true, to_apply=%add.2 | all-reduce | flops 1024 | bytes 4096
  1545.6 43.1 %all-gather.25.cloned.1.call-done = bf16[1312,1024]{0,1:T(8,128)(2,1)} async-done(((bf16[1312,64]{0,1:T(8,128)(2,1)}), bf16[1312,1024]{0,1:T(8,128)(2,1)}) %all-gather.25.cloned.1.call-update) | async-done | bytes 2686992 | tf_op jit(solution)/shard_map/all_gather | solution.py:250
  1593.7 41.7 %all-gather.19.cloned.1.call-done = bf16[512,3072]{0,1:T(8,128)(2,1)} async-done(((bf16[512,192]{0,1:T(8,128)(2,1)}), bf16[512,3072]{0,1:T(8,128)(2,1)}) %all-gather.19.cloned.1.call-update) | async-done | bytes 3145744 | tf_op jit(solution)/shard_map/all_gather | solution.py:241
  1640.8 53.0 %all-gather.23.cloned.1.call-done = bf16[512,5248]{0,1:T(8,128)(2,1)} async-done(((bf16[512,328]{0,1:T(8,128)(2,1)}), bf16[512,5248]{0,1:T(8,128)(2,1)}) %all-gather.23.cloned.1.call-update) | async-done | bytes 5373968 | tf_op jit(solution)/shard_map/all_gather | solution.py:247
  (494 shorter events, 454.3 us)
Async XLA Ops:
  7.2 85.5 %all-gather.11.cloned.1.call-start = ((), (), s32[]{:S(2)}) async-start(), calls=%async_computation.10 | async-start | bytes 9437184 | tf_op jit(solution)/shard_map/all_gather | solution.py:113
  7.9 293.9 %all-gather.13.cloned.1.call-start = ((), (), s32[]{:S(2)}) async-start(), calls=%async_computation.11 | async-start | bytes 3145728 | tf_op jit(solution)/shard_map/all_gather | solution.py:114
  8.7 295.9 %all-gather.15.cloned.1.call-start = ((), (), s32[]{:S(2)}) async-start(), calls=%async_computation.12 | async-start | bytes 16121856 | tf_op jit(solution)/shard_map/all_gather | solution.py:153
  9.4 323.4 %all-gather.17.cloned.1.call-start = ((), (), s32[]{:S(2)}) async-start(), calls=%async_computation.13 | async-start | bytes 8060928 | tf_op jit(solution)/shard_map/all_gather | solution.py:154
  10.0 817.6 %reduce-scatter.25.cloned.1.call-start = ((), (), s32[]{:S(2)}) async-start(), calls=%async_computation.16 | async-start | bytes 3145728 | tf_op jit(solution)/shard_map/reduce_scatter | solution.py:216
  359.1 471.4 %reduce-scatter.29.cloned.1.call-start = ((), (), s32[]{:S(2)}) async-start(), calls=%async_computation.20 | async-start | bytes 8060928 | tf_op jit(solution)/shard_map/reduce_scatter | solution.py:222
  369.2 523.6 %reduce-scatter.23.cloned.1.call-start = ((), (), s32[]{:S(2)}) async-start(), calls=%async_computation.14 | async-start | bytes 9437184 | tf_op jit(solution)/shard_map/reduce_scatter | solution.py:213
  380.9 29.1 %collective-permute-start.2 = (bf16[2,192,16,64]{1,3,2,0:T(8,128)(2,1)}, bf16[2,192,16,64]{1,3,2,0:T(8,128)(2,1)}, u32[]{:S(2)}, u32[]{:S(2)}) collective-permute-start(bf16[2,192,16,64]{1,3,2,0:T(8,128)(2,1)} %fusion.206), channel_id=1, source_target_pairs={{0,2},{2,4},{4,6},{6,8},{8,10},{10,12},{12,14},{14,0},{1,3},{3,5},... | collective-permute-start | bytes 2359304 | tf_op jit(solution)/shard_map/while/body/eval_jaxpr/ppermute | solution.py:16
  382.4 48.9 %collective-permute-start.1 = (bf16[2,192,16,64]{1,3,2,0:T(8,128)(2,1)S(1)}, bf16[2,192,16,64]{1,3,2,0:T(8,128)(2,1)}, u32[]{:S(2)}, u32[]{:S(2)}) collective-permute-start(bf16[2,192,16,64]{1,3,2,0:T(8,128)(2,1)S(1)} %copy.135), channel_id=1, source_target_pairs={{0,2},{2,4},{4,6},{6,8},{8,10},{10,12},{12,14},{14,0},{1,3},{3,5},... | collective-permute-start | bytes 2359304 | tf_op jit(solution)/shard_map/while/body/eval_jaxpr/ppermute | solution.py:16
  442.7 29.1 %collective-permute-start.2 = (bf16[2,192,16,64]{1,3,2,0:T(8,128)(2,1)}, bf16[2,192,16,64]{1,3,2,0:T(8,128)(2,1)}, u32[]{:S(2)}, u32[]{:S(2)}) collective-permute-start(bf16[2,192,16,64]{1,3,2,0:T(8,128)(2,1)} %fusion.206), channel_id=1, source_target_pairs={{0,2},{2,4},{4,6},{6,8},{8,10},{10,12},{12,14},{14,0},{1,3},{3,5},... | collective-permute-start | bytes 2359304 | tf_op jit(solution)/shard_map/while/body/eval_jaxpr/ppermute | solution.py:16
  442.7 49.5 %collective-permute-start.1 = (bf16[2,192,16,64]{1,3,2,0:T(8,128)(2,1)S(1)}, bf16[2,192,16,64]{1,3,2,0:T(8,128)(2,1)}, u32[]{:S(2)}, u32[]{:S(2)}) collective-permute-start(bf16[2,192,16,64]{1,3,2,0:T(8,128)(2,1)S(1)} %copy.135), channel_id=1, source_target_pairs={{0,2},{2,4},{4,6},{6,8},{8,10},{10,12},{12,14},{14,0},{1,3},{3,5},... | collective-permute-start | bytes 2359304 | tf_op jit(solution)/shard_map/while/body/eval_jaxpr/ppermute | solution.py:16
  503.4 29.1 %collective-permute-start.2 = (bf16[2,192,16,64]{1,3,2,0:T(8,128)(2,1)}, bf16[2,192,16,64]{1,3,2,0:T(8,128)(2,1)}, u32[]{:S(2)}, u32[]{:S(2)}) collective-permute-start(bf16[2,192,16,64]{1,3,2,0:T(8,128)(2,1)} %fusion.206), channel_id=1, source_target_pairs={{0,2},{2,4},{4,6},{6,8},{8,10},{10,12},{12,14},{14,0},{1,3},{3,5},... | collective-permute-start | bytes 2359304 | tf_op jit(solution)/shard_map/while/body/eval_jaxpr/ppermute | solution.py:16
  503.4 48.5 %collective-permute-start.1 = (bf16[2,192,16,64]{1,3,2,0:T(8,128)(2,1)S(1)}, bf16[2,192,16,64]{1,3,2,0:T(8,128)(2,1)}, u32[]{:S(2)}, u32[]{:S(2)}) collective-permute-start(bf16[2,192,16,64]{1,3,2,0:T(8,128)(2,1)S(1)} %copy.135), channel_id=1, source_target_pairs={{0,2},{2,4},{4,6},{6,8},{8,10},{10,12},{12,14},{14,0},{1,3},{3,5},... | collective-permute-start | bytes 2359304 | tf_op jit(solution)/shard_map/while/body/eval_jaxpr/ppermute | solution.py:16
  563.2 29.1 %collective-permute-start.2 = (bf16[2,192,16,64]{1,3,2,0:T(8,128)(2,1)}, bf16[2,192,16,64]{1,3,2,0:T(8,128)(2,1)}, u32[]{:S(2)}, u32[]{:S(2)}) collective-permute-start(bf16[2,192,16,64]{1,3,2,0:T(8,128)(2,1)} %fusion.206), channel_id=1, source_target_pairs={{0,2},{2,4},{4,6},{6,8},{8,10},{10,12},{12,14},{14,0},{1,3},{3,5},... | collective-permute-start | bytes 2359304 | tf_op jit(solution)/shard_map/while/body/eval_jaxpr/ppermute | solution.py:16
  563.2 47.6 %collective-permute-start.1 = (bf16[2,192,16,64]{1,3,2,0:T(8,128)(2,1)S(1)}, bf16[2,192,16,64]{1,3,2,0:T(8,128)(2,1)}, u32[]{:S(2)}, u32[]{:S(2)}) collective-permute-start(bf16[2,192,16,64]{1,3,2,0:T(8,128)(2,1)S(1)} %copy.135), channel_id=1, source_target_pairs={{0,2},{2,4},{4,6},{6,8},{8,10},{10,12},{12,14},{14,0},{1,3},{3,5},... | collective-permute-start | bytes 2359304 | tf_op jit(solution)/shard_map/while/body/eval_jaxpr/ppermute | solution.py:16
  622.0 29.1 %collective-permute-start.2 = (bf16[2,192,16,64]{1,3,2,0:T(8,128)(2,1)}, bf16[2,192,16,64]{1,3,2,0:T(8,128)(2,1)}, u32[]{:S(2)}, u32[]{:S(2)}) collective-permute-start(bf16[2,192,16,64]{1,3,2,0:T(8,128)(2,1)} %fusion.206), channel_id=1, source_target_pairs={{0,2},{2,4},{4,6},{6,8},{8,10},{10,12},{12,14},{14,0},{1,3},{3,5},... | collective-permute-start | bytes 2359304 | tf_op jit(solution)/shard_map/while/body/eval_jaxpr/ppermute | solution.py:16
  622.0 46.7 %collective-permute-start.1 = (bf16[2,192,16,64]{1,3,2,0:T(8,128)(2,1)S(1)}, bf16[2,192,16,64]{1,3,2,0:T(8,128)(2,1)}, u32[]{:S(2)}, u32[]{:S(2)}) collective-permute-start(bf16[2,192,16,64]{1,3,2,0:T(8,128)(2,1)S(1)} %copy.135), channel_id=1, source_target_pairs={{0,2},{2,4},{4,6},{6,8},{8,10},{10,12},{12,14},{14,0},{1,3},{3,5},... | collective-permute-start | bytes 2359304 | tf_op jit(solution)/shard_map/while/body/eval_jaxpr/ppermute | solution.py:16
  680.0 29.1 %collective-permute-start.2 = (bf16[2,192,16,64]{1,3,2,0:T(8,128)(2,1)}, bf16[2,192,16,64]{1,3,2,0:T(8,128)(2,1)}, u32[]{:S(2)}, u32[]{:S(2)}) collective-permute-start(bf16[2,192,16,64]{1,3,2,0:T(8,128)(2,1)} %fusion.206), channel_id=1, source_target_pairs={{0,2},{2,4},{4,6},{6,8},{8,10},{10,12},{12,14},{14,0},{1,3},{3,5},... | collective-permute-start | bytes 2359304 | tf_op jit(solution)/shard_map/while/body/eval_jaxpr/ppermute | solution.py:16
  680.0 45.8 %collective-permute-start.1 = (bf16[2,192,16,64]{1,3,2,0:T(8,128)(2,1)S(1)}, bf16[2,192,16,64]{1,3,2,0:T(8,128)(2,1)}, u32[]{:S(2)}, u32[]{:S(2)}) collective-permute-start(bf16[2,192,16,64]{1,3,2,0:T(8,128)(2,1)S(1)} %copy.135), channel_id=1, source_target_pairs={{0,2},{2,4},{4,6},{6,8},{8,10},{10,12},{12,14},{14,0},{1,3},{3,5},... | collective-permute-start | bytes 2359304 | tf_op jit(solution)/shard_map/while/body/eval_jaxpr/ppermute | solution.py:16
  736.9 29.1 %collective-permute-start.2 = (bf16[2,192,16,64]{1,3,2,0:T(8,128)(2,1)}, bf16[2,192,16,64]{1,3,2,0:T(8,128)(2,1)}, u32[]{:S(2)}, u32[]{:S(2)}) collective-permute-start(bf16[2,192,16,64]{1,3,2,0:T(8,128)(2,1)} %fusion.206), channel_id=1, source_target_pairs={{0,2},{2,4},{4,6},{6,8},{8,10},{10,12},{12,14},{14,0},{1,3},{3,5},... | collective-permute-start | bytes 2359304 | tf_op jit(solution)/shard_map/while/body/eval_jaxpr/ppermute | solution.py:16
  737.0 44.8 %collective-permute-start.1 = (bf16[2,192,16,64]{1,3,2,0:T(8,128)(2,1)S(1)}, bf16[2,192,16,64]{1,3,2,0:T(8,128)(2,1)}, u32[]{:S(2)}, u32[]{:S(2)}) collective-permute-start(bf16[2,192,16,64]{1,3,2,0:T(8,128)(2,1)S(1)} %copy.135), channel_id=1, source_target_pairs={{0,2},{2,4},{4,6},{6,8},{8,10},{10,12},{12,14},{14,0},{1,3},{3,5},... | collective-permute-start | bytes 2359304 | tf_op jit(solution)/shard_map/while/body/eval_jaxpr/ppermute | solution.py:16
  818.0 202.5 %reduce-scatter.27.cloned.1.call-start = ((), (), s32[]{:S(2)}) async-start(), calls=%async_computation.18 | async-start | bytes 16121856 | tf_op jit(solution)/shard_map/reduce_scatter | solution.py:219
  827.5 259.5 %reduce-scatter.35.cloned.1.call-start = ((), (), s32[]{:S(2)}) async-start(), calls=%async_computation.24 | async-start | bytes 2228224
  830.4 340.9 %reduce-scatter.41.cloned.1.call-start = ((), (), s32[]{:S(2)}) async-start(), calls=%async_computation.27 | async-start | bytes 6127616
  835.8 424.4 %reduce-scatter.33.cloned.1.call-start = ((), (), s32[]{:S(2)}) async-start(), calls=%async_computation.23 | async-start | bytes 6684672
  898.2 487.2 %reduce-scatter.39.cloned.1.call-start = ((), (), s32[]{:S(2)}) async-start(), calls=%async_computation.26 | async-start | bytes 11419648
  1029.0 415.9 %reduce-scatter.31.cloned.1.call-start = ((), (), s32[]{:S(2)}) async-start(), calls=%async_computation.22 | async-start | bytes 278528
  1042.6 460.6 %reduce-scatter.37.cloned.1.call-start = ((), (), s32[]{:S(2)}) async-start(), calls=%async_computation.25 | async-start | bytes 278528
  1043.6 499.4 %all-gather.21.cloned.1.call-start = ((), (), s32[]{:S(2)}) async-start(), calls=%async_computation.17 | async-start | bytes 1114112 | tf_op jit(solution)/shard_map/all_gather | solution.py:244
  1088.6 500.1 %all-gather.25.cloned.1.call-start = ((), (), s32[]{:S(2)}) async-start(), calls=%async_computation.21 | async-start | bytes 3063808 | tf_op jit(solution)/shard_map/all_gather | solution.py:250
  1173.1 462.3 %all-gather.19.cloned.1.call-start = ((), (), s32[]{:S(2)}) async-start(), calls=%async_computation.15 | async-start | bytes 3342336 | tf_op jit(solution)/shard_map/all_gather | solution.py:241
  1262.0 431.8 %all-gather.23.cloned.1.call-start = ((), (), s32[]{:S(2)}) async-start(), calls=%async_computation.19 | async-start | bytes 5709824 | tf_op jit(solution)/shard_map/all_gather | solution.py:247
  (117 other events, 2324.8 us)
Sparse Core Ops, SparseCore 0:
  9.5 83.0 all-gather.10
  94.2 33.1 all-gather.12
  128.9 132.3 all-gather.14
  262.7 70.0 all-gather.16
  359.2 31.8 reduce-scatter.24
  393.9 67.0 reduce-scatter.28
  818.2 74.6 reduce-scatter.22
  895.8 124.6 reduce-scatter.26
  1025.3 61.6 reduce-scatter.34
  1090.8 80.5 reduce-scatter.40
  1175.9 84.3 reduce-scatter.32
  1265.3 120.0 reduce-scatter.38
  1389.9 55.0 reduce-scatter.30
  1448.7 54.3 reduce-scatter.36
  1506.0 36.9 all-gather.20
  1545.3 43.3 all-gather.24
  1591.6 43.7 all-gather.18
  1638.3 55.4 all-gather.22
where the time goes:
time: 1720 us; the launch traced here: 1710 us
  waiting for transfers between devices  1300 us (76%)
  matrix products  166 us (10%)
  local copies, waits for them, and re-layouts  89.3 us (5%)
  other arithmetic  79.2 us (5%)
  blocking collectives  45.6 us (3%)
    unnamed x24, waiting for transfers between devices  447 us
    ppermute x22, waiting for transfers between devices, from_behind(): return lax.ppermute(value, axis, pairs)  444 us
    reduce_scatter x1, waiting for transfers between devices, local(): lax.psum_scatter(grad_in.astype(jnp.bfloat16), 'fsdp', scatter_dimension=...  122 us
    all_gather x1, waiting for transfers between devices, local(): lax.all_gather(qkv_weight, 'fsdp', axis=0, tiled=True)  70.4 us
    unnamed x141, local copies, waits for them, and re-layouts  60.3 us
    reduce_scatter x1, waiting for transfers between devices, local(): lax.psum_scatter(grad_wqkv.astype(jnp.bfloat16), 'fsdp', scatter_dimensio...  56.9 us
    all_gather x1, waiting for transfers between devices, local(): lax.all_gather(pieces[2].astype(jnp.bfloat16), ('dp', 'ctx'), axis=1, til...  53 us
    all_gather x1, waiting for transfers between devices, local(): lax.all_gather(pieces[3].astype(jnp.bfloat16), ('dp', 'ctx'), axis=1, til...  43.1 us
  transfers between devices with their start and end apart: 40, of which 36 were waited for; matrix products, arithmetic and copies ran while one was open for 17% of the time, Pallas kernels for 0%

commit v1 on v0

v1 whole, which is shorter than its diff:
```python
import jax
import jax.numpy as jnp
from jax import lax
from jax.sharding import PartitionSpec as P

HEAD_DIM = 64
LONGEST_UNROLLED = 8


theta_base = 160000.0
epsilon = 1e-05


def layer_norm(values, gain):
    centred = values - jnp.mean(values, -1, keepdims=True)
    spread = jnp.mean(centred * centred, -1, keepdims=True)
    return centred * lax.rsqrt(spread + epsilon) * gain


def rope_tables(positions, head_size):
    middle = head_size // 2
    inverse = theta_base ** (-(jnp.arange(middle).astype(jnp.float32) * 2.0) / head_size)
    angles = positions[:, None] * inverse[None, :]
    cosine = jnp.cos(angles)
    sine = jnp.sin(angles)
    return (jnp.concatenate([cosine, cosine], -1), jnp.concatenate([sine, sine], -1))


def rotate(values, cosine, sine):
    middle = values.shape[-1] // 2
    turned = jnp.concatenate([-values[..., middle:], values[..., :middle]], -1)
    return values * cosine[:, None, :] + turned * sine[:, None, :]


def unrotate(grads_in, cosine, sine):
    middle = grads_in.shape[-1] // 2
    scaled = grads_in * sine[:, None, :]
    return grads_in * cosine[:, None, :] + jnp.concatenate(
        [scaled[..., middle:], -scaled[..., :middle]], -1
    )


def geglu(expanded):
    middle = expanded.shape[-1] // 2
    return jax.nn.gelu(expanded[:, :middle], approximate=False) * expanded[:, middle:]


def ring_place(index, count):
    return index // 2 if index % 2 == 0 else count - 1 - index // 2


def ring_pairs(count, steps):
    at = sorted(range(count), key=lambda index: ring_place(index, count))
    return [(at[place], at[(place + steps) % count]) for place in range(count)]


def along_ring(value, steps):
    return lax.ppermute(value, "ctx", ring_pairs(lax.axis_size("ctx"), steps))


def swap(value, axis):
    return lax.ppermute(value, axis, [(0, 1), (1, 0)])


def fetch_rows(shard):
    part = shard.shape[0] // 2
    half = lax.dynamic_slice_in_dim(shard, lax.axis_index("dp") * part, part, 0)
    return lax.all_gather(swap(half, "fsdp"), "dp", axis=0, tiled=True)


def halves_of(values, first):
    middle = values.shape[1] // 2
    low, high = values[:, :middle], values[:, middle:]
    return jnp.where(first, low, high), jnp.where(first, high, low)


def join_halves(own, other, first):
    return jnp.where(first, jnp.concatenate([own, other], 1), jnp.concatenate([other, own], 1))


def dot_rows(values, own, other, first):
    mine, others = halves_of(values, first)
    return jnp.dot(mine, own, preferred_element_type=jnp.float32) + jnp.dot(
        others, other, preferred_element_type=jnp.float32
    )


def dot_rows_back(grads, own, other, first):
    mine = jnp.einsum("tg,fg->tf", grads, own, preferred_element_type=jnp.float32)
    others = jnp.einsum("tg,fg->tf", grads, other, preferred_element_type=jnp.float32)
    return join_halves(mine, others, first)


def add_low(left, right):
    return (left.astype(jnp.float32) + right.astype(jnp.float32)).astype(jnp.bfloat16)


def pick(values, number, axis):
    return lax.dynamic_index_in_dim(values, number, axis, keepdims=False)


def reduce_rows(grads):
    rows, columns = grads.shape
    core, shard = lax.axis_index("dp"), lax.axis_index("fsdp")
    quarters = grads.astype(jnp.bfloat16).reshape(2, 2, rows // 4, columns)
    summed = add_low(pick(quarters, core, 1), swap(pick(quarters, 1 - core, 1), "dp"))
    summed = add_low(pick(summed, shard, 0), swap(pick(summed, 1 - shard, 0), "fsdp"))
    if summed.shape[0] % (lax.axis_size("ctx") * 8):
        summed = summed.reshape(-1, 128)
    piece = lax.psum_scatter(summed, "ctx", scatter_dimension=0, tiled=True)
    shared = lax.all_gather(piece, ("dp", "ctx"), axis=0, tiled=True)
    return shared.reshape(rows // 2, columns).astype(jnp.float32)


def attend_block(queries, paired, state, scale):
    best, total, summed = state
    scores = (
        jnp.einsum("qhe,khe->hqk", queries, paired[0], preferred_element_type=jnp.float32) * scale
    )
    peak = jnp.maximum(best, jnp.max(scores, -1))
    shrink = jnp.exp(best - peak)
    weights = jnp.exp(scores - peak[..., None])
    total = total * shrink + jnp.sum(weights, -1)
    update = jnp.einsum(
        "hqk,khe->qhe", weights.astype(jnp.bfloat16), paired[1], preferred_element_type=jnp.float32
    )
    summed = summed * jnp.transpose(shrink)[:, :, None] + update
    return (peak, total, summed)


def back_block(queries, grad_attended, log_total, delta, paired, grad_queries, scale):
    scores = (
        jnp.einsum("qhe,khe->hqk", queries, paired[0], preferred_element_type=jnp.float32) * scale
    )
    probs = jnp.exp(scores - log_total[..., None])
    grad_probs = jnp.einsum(
        "qhe,khe->hqk", grad_attended, paired[1], preferred_element_type=jnp.float32
    )
    grad_scores = (probs * (grad_probs - delta[..., None])).astype(jnp.bfloat16)
    grad_values = jnp.einsum(
        "hqk,qhe->khe",
        probs.astype(jnp.bfloat16),
        grad_attended,
        preferred_element_type=jnp.float32,
    )
    grad_keys = (
        jnp.einsum("hqk,qhe->khe", grad_scores, queries, preferred_element_type=jnp.float32) * scale
    )
    grad_queries = (
        grad_queries
        + jnp.einsum("hqk,khe->qhe", grad_scores, paired[0], preferred_element_type=jnp.float32)
        * scale
    )
    return (jnp.stack([grad_keys, grad_values]), grad_queries)


def local(tokens, attn_gain, qkv_weight, out_weight, mlp_gain, in_weight, down_weight, cotangent):
    row_count = tokens.shape[1]
    cycle_size = lax.axis_size("ctx")
    first = lax.axis_index("fsdp") == 0
    gains = jnp.stack([attn_gain, mlp_gain]).astype(jnp.float32)
    gains = join_halves(gains, swap(gains, "fsdp"), first)
    gain_att, gain_mlp = gains[0], gains[1]
    other_qkv = fetch_rows(qkv_weight)
    other_out = fetch_rows(out_weight)
    other_in = fetch_rows(in_weight)
    other_down = fetch_rows(down_weight)
    width = out_weight.shape[1]
    head_size = HEAD_DIM
    heads = width // head_size
    shaped = (row_count, heads, head_size)
    scale = head_size ** (-0.5)
    inputs = tokens[0].astype(jnp.float32)
    positions = (lax.axis_index("ctx") * row_count + jnp.arange(row_count, dtype=jnp.int32)).astype(
        jnp.float32
    )
    cosine, sine = rope_tables(positions, head_size)
    normed = layer_norm(inputs, gain_att).astype(jnp.bfloat16)
    projected = dot_rows(normed, qkv_weight, other_qkv, first)
    queries = rotate(projected[:, :width].reshape(shaped), cosine, sine).astype(jnp.bfloat16)
    keys = rotate(projected[:, width : 2 * width].reshape(shaped), cosine, sine).astype(
        jnp.bfloat16
    )
    values = projected[:, 2 * width :].astype(jnp.bfloat16)
    local_pair = jnp.concatenate([keys.reshape(row_count, width), values], 1)

    def as_heads(blocks):
        joined = jnp.concatenate(blocks, 0)
        split = joined.reshape(joined.shape[0], 2, heads, head_size)
        return (split[:, 0], split[:, 1])

    state = (
        jnp.full((heads, row_count), -1e30, jnp.float32),
        jnp.zeros((heads, row_count), jnp.float32),
        jnp.zeros(shaped, jnp.float32),
    )
    unrolled = cycle_size <= LONGEST_UNROLLED
    groups = [[local_pair]]
    if unrolled:
        before, after = local_pair, local_pair
        for step in range(1, cycle_size // 2 + 1):
            before = along_ring(before, 1)
            group = [before]
            if step < cycle_size // 2:
                after = along_ring(after, -1)
                group.append(after)
            state = attend_block(queries, as_heads(groups[-1]), state, scale)
            groups.append(group)
        best, total, summed = attend_block(queries, as_heads(groups[-1]), state, scale)
    else:

        def forward_turn(number, carry):
            state, paired = carry
            return (
                attend_block(queries, as_heads([paired]), state, scale),
                along_ring(paired, 1),
            )

        state, paired = lax.fori_loop(0, cycle_size - 1, forward_turn, (state, local_pair))
        best, total, summed = attend_block(queries, as_heads([paired]), state, scale)
    attended = summed / jnp.transpose(total)[:, :, None]
    log_total = best + jnp.log(total)
    attended_low = attended.reshape(row_count, width).astype(jnp.bfloat16)
    residual = inputs + dot_rows(attended_low, out_weight, other_out, first)
    normed_mlp = layer_norm(residual, gain_mlp).astype(jnp.bfloat16)
    expanded = dot_rows(normed_mlp, in_weight, other_in, first)
    gated = geglu(expanded).astype(jnp.bfloat16)
    output = residual + dot_rows(gated, down_weight, other_down, first)
    grad_output = cotangent[0]
    grad_down = jnp.einsum("tf,td->fd", gated, grad_output, preferred_element_type=jnp.float32)
    grad_gated = dot_rows_back(grad_output, down_weight, other_down, first)
    unused_gate, pull_gate = jax.vjp(geglu, expanded)
    grad_expanded = pull_gate(grad_gated)[0].astype(jnp.bfloat16)
    grad_in = jnp.einsum("tf,tg->fg", normed_mlp, grad_expanded, preferred_element_type=jnp.float32)
    grad_normed_mlp = dot_rows_back(grad_expanded, in_weight, other_in, first)
    unused_mlp, pull_mlp = jax.vjp(layer_norm, residual, gain_mlp)
    grad_residual_mlp, grad_gain_mlp = pull_mlp(grad_normed_mlp)
    grad_residual = grad_output.astype(jnp.float32) + grad_residual_mlp
    grad_branch = grad_residual.astype(jnp.bfloat16)
    grad_wout = jnp.einsum(
        "tf,td->fd", attended_low, grad_branch, preferred_element_type=jnp.float32
    )
    grad_attended = (
        dot_rows_back(grad_branch, out_weight, other_out, first).astype(jnp.bfloat16).reshape(shaped)
    )
    delta = jnp.einsum("qhe,qhe->hq", grad_attended.astype(jnp.float32), attended)

    grad_queries = jnp.zeros(shaped, jnp.float32)

    def back_pair(blocks, grad_queries):
        grad_pair, grad_queries = back_block(
            queries, grad_attended, log_total, delta, as_heads(blocks), grad_queries, scale
        )
        return jnp.transpose(grad_pair, (1, 0, 2, 3)).reshape(-1, 2 * width), grad_queries

    if unrolled:
        forth, back = None, None
        for step in range(cycle_size // 2, -1, -1):
            grad_pair, grad_queries = back_pair(groups[step], grad_queries)
            if step == 0:
                grad_pair = grad_pair + forth.astype(jnp.float32) + back.astype(jnp.float32)
                break
            if step == cycle_size // 2:
                forth = along_ring(grad_pair.astype(jnp.bfloat16), 1)
                continue
            ahead = grad_pair[row_count:] + forth.astype(jnp.float32)
            behind = grad_pair[:row_count]
            if back is not None:
                behind = behind + back.astype(jnp.float32)
            forth = along_ring(ahead.astype(jnp.bfloat16), 1)
            back = along_ring(behind.astype(jnp.bfloat16), -1)
    else:

        def backward_turn(number, carry):
            paired_now, sent, grad_queries = carry
            grad_pair, grad_queries = back_pair([paired_now], grad_queries)
            grad_pair = (grad_pair + sent.astype(jnp.float32)).astype(jnp.bfloat16)
            return (along_ring(paired_now, 1), along_ring(grad_pair, 1), grad_queries)

        start_back = (local_pair, jnp.zeros_like(local_pair), grad_queries)
        unused_pair, sent, grad_queries = lax.fori_loop(
            0, cycle_size, backward_turn, start_back
        )
        grad_pair = sent.astype(jnp.float32)
    grad_projected = jnp.concatenate(
        [
            unrotate(grad_queries, cosine, sine).reshape(row_count, width),
            unrotate(grad_pair[:, :width].reshape(shaped), cosine, sine).reshape(row_count, width),
            grad_pair[:, width:],
        ],
        1,
    ).astype(jnp.bfloat16)
    grad_wqkv = jnp.einsum("tf,tg->fg", normed, grad_projected, preferred_element_type=jnp.float32)
    grad_normed = dot_rows_back(grad_projected, qkv_weight, other_qkv, first)
    unused_att, pull_att = jax.vjp(layer_norm, inputs, gain_att)
    grad_inputs_att, grad_gain_att = pull_att(grad_normed)
    grad_inputs = grad_residual + grad_inputs_att
    grad_gains = lax.psum(jnp.stack([grad_gain_att, grad_gain_mlp]), ("dp", "ctx", "fsdp"))
    grad_gains, unused_half = halves_of(grad_gains, first)
    return (
        output.astype(jnp.bfloat16)[None],
        grad_inputs[None],
        grad_gains[0],
        reduce_rows(grad_wqkv),
        reduce_rows(grad_wout),
        grad_gains[1],
        reduce_rows(grad_in),
        reduce_rows(grad_down),
    )


def solution(mesh):
    in_specs = (
        P(("dp", "fsdp"), "ctx", None),
        P("fsdp"),
        P("fsdp", None),
        P("fsdp", None),
        P("fsdp"),
        P("fsdp", None),
        P("fsdp", None),
        P(("dp", "fsdp"), "ctx", None),
    )
    out_specs = (
        P(("dp", "fsdp"), "ctx", None),
        P(("dp", "fsdp"), "ctx", None),
        P("fsdp"),
        P("fsdp", None),
        P("fsdp", None),
        P("fsdp"),
        P("fsdp", None),
        P("fsdp", None),
    )
    return jax.shard_map(local, mesh=mesh, in_specs=in_specs, out_specs=out_specs, check_vma=False)
```

time: 1720 us -> 933 us (0.54)
  waiting for transfers between devices: 1300 us -> 504 us
  matrix products: 166 us -> 114 us
  local copies, waits for them, and re-layouts: 89.3 us -> 120 us
  starting transfers between devices: 6.23 us -> 28.6 us
  other arithmetic: 79.2 us -> 101 us
    unnamed x24 -> x12, waiting for transfers between devices: 447 us -> 1.33 us
    ppermute x22 -> x27, waiting for transfers between devices: 444 us -> 253 us  [the longest x13 200 us: swap(): return lax.ppermute(value, axis, [(0, 1), (1, 0)])]
    all_gather x8, waiting for transfers between devices: 234 us -> 119 us  [the longest x4 119 us: reduce_rows(): shared = lax.all_gather(piece, ('dp', 'ctx'), axis=0, tiled=True)]
    reduce_scatter x4, waiting for transfers between devices: 179 us -> 130 us  [reduce_rows(): piece = lax.psum_scatter(summed, 'ctx', scatter_dimension=0, tiled=True)]
    psum x0 -> x1, blocking collectives: none -> 39.8 us  [local(): lax.psum(jnp.stack([grad_gain_att, grad_gain_mlp]), ('dp', 'ctx', 'fsdp'))]
    unnamed x2 -> x0, blocking collectives: 36 us -> none
    unnamed x141 -> x280, local copies, waits for them, and re-layouts: 60.3 us -> 25.5 us
    slice x2 -> x16, local copies, waits for them, and re-layouts: 0.25 us -> 28.5 us  [the longest x6 15.7 us: local(): ahead = grad_pair[row_count:] + forth.astype(jnp.float32)]
  transfers between devices with their start and end apart: 40 -> 39, of which waited for: 36 -> 18; matrix products, arithmetic and copies ran while one was open for 17% -> 27% of each run, Pallas kernels for 0% -> 0%
where the time goes in v1:
time: 933 us; the launch traced here: 923 us
  waiting for transfers between devices  504 us (54%)
  local copies, waits for them, and re-layouts  120 us (13%)
  matrix products  114 us (12%)
  other arithmetic  101 us (11%)
  blocking collectives  39.8 us (4%)
  starting transfers between devices  28.6 us (3%)
  between operations  16.3 us (2%)
    ppermute x13, waiting for transfers between devices, swap(): return lax.ppermute(value, axis, [(0, 1), (1, 0)])  200 us
    reduce_scatter x4, waiting for transfers between devices, reduce_rows(): piece = lax.psum_scatter(summed, 'ctx', scatter_dimension=0, tiled=True)  130 us
    all_gather x4, waiting for transfers between devices, reduce_rows(): shared = lax.all_gather(piece, ('dp', 'ctx'), axis=0, tiled=True)  119 us
    ppermute x14, waiting for transfers between devices, along_ring(): return lax.ppermute(value, 'ctx', ring_pairs(lax.axis_size('ctx'), steps))  53.5 us
    psum x1, blocking collectives, local(): lax.psum(jnp.stack([grad_gain_att, grad_gain_mlp]), ('dp', 'ctx', 'fsdp'))  39.8 us
    convert_element_type x8, other arithmetic, add_low(): (left.astype(jnp.float32) + right.astype(jnp.float32)).astype(jnp.bfloat16)  28.6 us
    unnamed x280, local copies, waits for them, and re-layouts  25.5 us
    dot_general x5, matrix products, attend_block(): jnp.einsum('qhe,khe->hqk', queries, paired[0], preferred_element_type=jnp...  19 us
  transfers between devices with their start and end apart: 39, of which 18 were waited for; matrix products, arithmetic and copies ran while one was open for 27% of the time, Pallas kernels for 0%

profile of v1, /device:TPU:0, one launch (start us, length us, event | category | flops | bytes accessed | tf_op | source)
XLA Modules:
  0.0 923.4 jit_solution(3061001982723081834)
XLA Ops:
  12.2 34.5 %collective-permute-done.1 = bf16[256,3072]{1,0:T(8,128)(2,1)} collective-permute-done((bf16[256,3072]{1,0:T(8,128)(2,1)S(1)}, bf16[256,3072]{1,0:T(8,128)(2,1)}, u32[]{:S(2)}, u32[]{:S(2)}) %collective-permute-start.1) | collective-permute-done | bytes 1572896 | tf_op jit(solution)/shard_map/ppermute | solution.py:62
  53.1 27.8 %collective-permute-done.11 = bf16[656,1024]{1,0:T(8,128)(2,1)} collective-permute-done((bf16[656,1024]{1,0:T(8,128)(2,1)S(1)}, bf16[656,1024]{1,0:T(8,128)(2,1)}, u32[]{:S(2)}, u32[]{:S(2)}) %collective-permute-start.11) | collective-permute-done | bytes 1343520 | tf_op jit(solution)/shard_map/ppermute | solution.py:62
  119.2 4.0 fusion.177
  123.2 24.8 %collective-permute-done.10 = bf16[256,5248]{1,0:T(8,128)(2,1)} collective-permute-done((bf16[256,5248]{1,0:T(8,128)(2,1)}, bf16[256,5248]{1,0:T(8,128)(2,1)}, u32[]{:S(2)}, u32[]{:S(2)}) %collective-permute-start.10) | collective-permute-done | bytes 2687008 | tf_op jit(solution)/shard_map/ppermute | solution.py:62
  166.7 10.1 %collective-permute-done.4 = bf16[192,2048]{1,0:T(8,128)(2,1)} collective-permute-done((bf16[192,2048]{1,0:T(8,128)(2,1)}, bf16[192,2048]{1,0:T(8,128)(2,1)}, u32[]{:S(2)}, u32[]{:S(2)}) %collective-permute-start.4) | collective-permute-done | bytes 786464 | tf_op jit(solution)/shard_map/ppermute | solution.py:58
  184.1 4.9 multiply_reduce_fusion.2
  195.6 4.9 multiply_reduce_fusion.1
  205.8 4.9 multiply_reduce_fusion
  245.7 5.7 fusion.180
  251.4 5.3 convolution_add_fusion
  256.8 4.8 fusion.141
  297.3 5.8 convolution_convert_fusion
  351.5 5.4 dynamic-slice_bitcast_fusion
  366.8 15.0 %collective-permute-done.13 = bf16[192,2048]{1,0:T(8,128)(2,1)S(1)} collective-permute-done((bf16[192,2048]{1,0:T(8,128)(2,1)S(1)}, bf16[192,2048]{1,0:T(8,128)(2,1)S(1)}, u32[]{:S(2)}, u32[]{:S(2)}) %collective-permute-start.13) | collective-permute-done | bytes 786464 | tf_op jit(solution)/shard_map/ppermute | solution.py:58
  386.5 14.4 %collective-permute-done.14 = bf16[192,2048]{1,0:T(8,128)(2,1)S(1)} collective-permute-done((bf16[192,2048]{1,0:T(8,128)(2,1)S(1)}, bf16[192,2048]{1,0:T(8,128)(2,1)S(1)}, u32[]{:S(2)}, u32[]{:S(2)}) %collective-permute-start.14) | collective-permute-done | bytes 786464 | tf_op jit(solution)/shard_map/ppermute | solution.py:58
  408.6 12.0 %collective-permute-done.15 = bf16[192,2048]{1,0:T(8,128)(2,1)} collective-permute-done((bf16[192,2048]{1,0:T(8,128)(2,1)}, bf16[192,2048]{1,0:T(8,128)(2,1)}, u32[]{:S(2)}, u32[]{:S(2)}) %collective-permute-start.15) | collective-permute-done | bytes 786464 | tf_op jit(solution)/shard_map/ppermute | solution.py:58
  444.1 6.4 collective-permute-done.22
  452.8 26.1 %collective-permute-done.26 = bf16[656,1024]{1,0:T(8,128)(2,1)} collective-permute-done((bf16[656,1024]{1,0:T(8,128)(2,1)}, bf16[656,1024]{1,0:T(8,128)(2,1)}, u32[]{:S(2)}, u32[]{:S(2)}) %collective-permute-start.26) | collective-permute-done | bytes 1343520 | tf_op jit(solution)/shard_map/ppermute | solution.py:62
  485.7 4.0 fusion.1
  491.8 5.4 fusion
  501.6 27.0 %collective-permute-done.20 = bf16[256,3072]{1,0:T(8,128)(2,1)} collective-permute-done((bf16[256,3072]{1,0:T(8,128)(2,1)}, bf16[256,3072]{1,0:T(8,128)(2,1)}, u32[]{:S(2)}, u32[]{:S(2)}) %collective-permute-start.20) | collective-permute-done | bytes 1572896 | tf_op jit(solution)/shard_map/ppermute | solution.py:62
  531.8 53.1 %collective-permute-done.24 = bf16[256,5248]{1,0:T(8,128)(2,1)} collective-permute-done((bf16[256,5248]{1,0:T(8,128)(2,1)}, bf16[256,5248]{1,0:T(8,128)(2,1)}, u32[]{:S(2)}, u32[]{:S(2)}) %collective-permute-start.24) | collective-permute-done | bytes 2687008 | tf_op jit(solution)/shard_map/ppermute | solution.py:62
  584.9 4.7 fusion.3
  591.0 56.1 %reduce-scatter.5.cloned.1.call-done = bf16[32,3072]{1,0:T(8,128)(2,1)} async-done(((bf16[256,3072]{1,0:T(8,128)(2,1)}), bf16[32,3072]{1,0:T(8,128)(2,1)}) %reduce-scatter.5.cloned.1.call-update) | async-done | bytes 196624 | tf_op jit(solution)/shard_map/reduce_scatter | solution.py:110
  647.3 73.7 %reduce-scatter.9.cloned.1.call-done = bf16[32,5248]{1,0:T(8,128)(2,1)} async-done(((bf16[256,5248]{1,0:T(8,128)(2,1)}), bf16[32,5248]{1,0:T(8,128)(2,1)}) %reduce-scatter.9.cloned.1.call-update) | async-done | bytes 335888 | tf_op jit(solution)/shard_map/reduce_scatter | solution.py:110
  730.9 39.8 %psum.7 = f32[2,1024]{1,0:T(2,128)S(1)} all-reduce(f32[2,1024]{1,0:T(2,128)} %pad_maximum_fusion.10), channel_id=1, replica_groups=mesh['dp'=2,'ctx'=8,'fsdp'=2] {'dp','ctx','fsdp'}, use_global_device_ids=true, to_apply=%region_20.21 | all-reduce | flops 2048 | bytes 16384 | tf_op jit(solution)/shard_map/psum | solution.py:298
  778.7 26.2 %all-gather.23.cloned.1.call-done = bf16[10496,128]{1,0:T(8,128)(2,1)} async-done(((bf16[656,128]{1,0:T(8,128)(2,1)}), bf16[10496,128]{1,0:T(8,128)(2,1)}) %all-gather.23.cloned.1.call-update) | async-done | bytes 2686992 | tf_op jit(solution)/shard_map/all_gather | solution.py:111
  805.0 5.6 reshape.297
  810.5 40.8 %all-gather.17.cloned.1.call-done = bf16[512,3072]{1,0:T(8,128)(2,1)} async-done(((bf16[32,3072]{1,0:T(8,128)(2,1)}), bf16[512,3072]{1,0:T(8,128)(2,1)}) %all-gather.17.cloned.1.call-update) | async-done | bytes 3145744 | tf_op jit(solution)/shard_map/all_gather | solution.py:111
  851.3 5.4 convert_element_type.335
  856.7 52.2 %all-gather.21.cloned.1.call-done = bf16[512,5248]{1,0:T(8,128)(2,1)} async-done(((bf16[32,5248]{1,0:T(8,128)(2,1)}), bf16[512,5248]{1,0:T(8,128)(2,1)}) %all-gather.21.cloned.1.call-update) | async-done | bytes 5373968 | tf_op jit(solution)/shard_map/all_gather | solution.py:111
  908.9 7.4 convert_element_type.355
  (520 shorter events, 288.7 us)
Async XLA Ops:
  7.2 89.2 %all-gather.9.cloned.1.call-start = ((), (), s32[]{:S(2)}) async-start(), calls=%async_computation.4 | async-start | bytes 4718592 | tf_op jit(solution)/shard_map/all_gather | solution.py:68
  9.2 37.5 %collective-permute-start.1 = (bf16[256,3072]{1,0:T(8,128)(2,1)S(1)}, bf16[256,3072]{1,0:T(8,128)(2,1)}, u32[]{:S(2)}, u32[]{:S(2)}) collective-permute-start(bf16[256,3072]{1,0:T(8,128)(2,1)S(1)} %constant_dynamic-slice_fusion.3), channel_id=1, source_target_pairs={{0,1},{1,0},{2,3},{3,2},{4,5},{5,4},{6,7},{7,6},{8,9},{9,8},{10,11... | collective-permute-start | bytes 4718600 | tf_op jit(solution)/shard_map/ppermute | solution.py:62
  46.7 101.4 %all-gather.15.cloned.1.call-start = ((), (), s32[]{:S(2)}) async-start(), calls=%async_computation.7 | async-start | bytes 4030464 | tf_op jit(solution)/shard_map/all_gather | solution.py:68
  48.3 32.6 %collective-permute-start.11 = (bf16[656,1024]{1,0:T(8,128)(2,1)S(1)}, bf16[656,1024]{1,0:T(8,128)(2,1)}, u32[]{:S(2)}, u32[]{:S(2)}) collective-permute-start(bf16[656,1024]{1,0:T(8,128)(2,1)S(1)} %constant_dynamic-slice_fusion), channel_id=1, source_target_pairs={{0,1},{1,0},{2,3},{3,2},{4,5},{5,4},{6,7},{7,6},{8,9},{9,8},{10,11... | collective-permute-start | bytes 4030472 | tf_op jit(solution)/shard_map/ppermute | solution.py:62
  50.2 42.4 %collective-permute-start = (f32[2,512]{1,0:T(2,128)S(1)}, f32[2,512]{1,0:T(2,128)S(1)}, u32[]{:S(2)}, u32[]{:S(2)}) collective-permute-start(f32[2,512]{1,0:T(2,128)S(1)} %maximum_convert_fusion), channel_id=1, source_target_pairs={{0,1},{1,0},{2,3},{3,2},{4,5},{5,4},{6,7},{7,6},{8,9},{9,8},{10,11... | collective-permute-start | bytes 12296 | tf_op jit(solution)/shard_map/ppermute | solution.py:62
  51.3 44.9 %collective-permute-start.9 = (bf16[256,1024]{1,0:T(8,128)(2,1)}, bf16[256,1024]{1,0:T(8,128)(2,1)}, u32[]{:S(2)}, u32[]{:S(2)}) collective-permute-start(bf16[256,1024]{1,0:T(8,128)(2,1)} %constant_dynamic-slice_fusion.2), channel_id=1, source_target_pairs={{0,1},{1,0},{2,3},{3,2},{4,5},{5,4},{6,7},{7,6},{8,9},{9,8},{10,11... | collective-permute-start | bytes 1572872 | tf_op jit(solution)/shard_map/ppermute | solution.py:62
  80.9 160.7 %all-gather.11.cloned.1.call-start = ((), (), s32[]{:S(2)}) async-start(), calls=%async_computation.5 | async-start | bytes 1572864 | tf_op jit(solution)/shard_map/all_gather | solution.py:68
  84.5 63.6 %collective-permute-start.10 = (bf16[256,5248]{1,0:T(8,128)(2,1)}, bf16[256,5248]{1,0:T(8,128)(2,1)}, u32[]{:S(2)}, u32[]{:S(2)}) collective-permute-start(bf16[256,5248]{1,0:T(8,128)(2,1)} %constant_dynamic-slice_fusion.1), channel_id=1, source_target_pairs={{0,1},{1,0},{2,3},{3,2},{4,5},{5,4},{6,7},{7,6},{8,9},{9,8},{10,11... | collective-permute-start | bytes 8060936 | tf_op jit(solution)/shard_map/ppermute | solution.py:62
  96.3 155.2 %all-gather.13.cloned.1.call-start = ((), (), s32[]{:S(2)}) async-start(), calls=%async_computation.6 | async-start | bytes 8060928 | tf_op jit(solution)/shard_map/all_gather | solution.py:68
  117.1 41.5 %collective-permute-start.2 = (bf16[192,2048]{1,0:T(8,128)(2,1)}, bf16[192,2048]{1,0:T(8,128)(2,1)}, u32[]{:S(2)}, u32[]{:S(2)}) collective-permute-start(bf16[192,2048]{1,0:T(8,128)(2,1)} %pad_maximum_fusion.7), channel_id=1, source_target_pairs={{0,4},{4,8},{8,12},{12,14},{14,10},{10,6},{6,2},{2,0},{1,5},{5,9},... | collective-permute-start | bytes 2359304 | tf_op jit(solution)/shard_map/ppermute | solution.py:58
  118.8 43.0 %collective-permute-start.3 = (bf16[192,2048]{1,0:T(8,128)(2,1)}, bf16[192,2048]{1,0:T(8,128)(2,1)}, u32[]{:S(2)}, u32[]{:S(2)}) collective-permute-start(bf16[192,2048]{1,0:T(8,128)(2,1)} %pad_maximum_fusion.7), channel_id=1, source_target_pairs={{0,2},{4,0},{8,4},{12,8},{14,12},{10,14},{6,10},{2,6},{1,3},{5,1},... | collective-permute-start | bytes 2359304 | tf_op jit(solution)/shard_map/ppermute | solution.py:58
  148.1 441.6 %reduce-scatter.7.cloned.1.call-start = ((), (), s32[]{:S(2)}) async-start(), calls=%async_computation.10 | async-start | bytes 589824 | tf_op jit(solution)/shard_map/reduce_scatter | solution.py:110
  161.8 21.4 %collective-permute-start.5 = (bf16[192,2048]{1,0:T(8,128)(2,1)}, bf16[192,2048]{1,0:T(8,128)(2,1)}, u32[]{:S(2)}, u32[]{:S(2)}) collective-permute-start(bf16[192,2048]{1,0:T(8,128)(2,1)} %collective-permute-done.3), channel_id=1, source_target_pairs={{0,2},{4,0},{8,4},{12,8},{14,12},{10,14},{6,10},{2,6},{1,3},{5,1},... | collective-permute-start | bytes 2359304 | tf_op jit(solution)/shard_map/ppermute | solution.py:58
  307.2 52.9 %collective-permute-start.12 = (bf16[192,2048]{1,0:T(8,128)(2,1)}, bf16[192,2048]{1,0:T(8,128)(2,1)}, u32[]{:S(2)}, u32[]{:S(2)}) collective-permute-start(bf16[192,2048]{1,0:T(8,128)(2,1)} %copy.157), channel_id=1, source_target_pairs={{0,4},{4,8},{8,12},{12,14},{14,10},{10,6},{6,2},{2,0},{1,5},{5,9},... | collective-permute-start | bytes 2359304 | tf_op jit(solution)/shard_map/ppermute | solution.py:58
  310.6 122.0 %collective-permute-start.21 = (bf16[2,256,1024]{2,1,0:T(8,128)(2,1)}, bf16[2,256,1024]{2,1,0:T(8,128)(2,1)}, u32[]{:S(2)}, u32[]{:S(2)}) collective-permute-start(bf16[2,256,1024]{2,1,0:T(8,128)(2,1)} %dynamic-slice_bitcast_fusion.6), channel_id=1, source_target_pairs={{0,16},{16,0},{1,17},{17,1},{2,18},{18,2},{3,19},{19,3},{4,20},{20... | collective-permute-start | bytes 3145736 | tf_op jit(solution)/shard_map/ppermute | solution.py:62
  318.4 45.1 %collective-permute-start.16 = (bf16[192,2048]{1,0:T(8,128)(2,1)}, bf16[192,2048]{1,0:T(8,128)(2,1)}, u32[]{:S(2)}, u32[]{:S(2)}) collective-permute-start(bf16[192,2048]{1,0:T(8,128)(2,1)} %copy.162), channel_id=1, source_target_pairs={{0,2},{4,0},{8,4},{12,8},{14,12},{10,14},{6,10},{2,6},{1,3},{5,1},... | collective-permute-start | bytes 2359304 | tf_op jit(solution)/shard_map/ppermute | solution.py:58
  351.4 84.9 %collective-permute-start.25 = (bf16[2,656,1024]{2,1,0:T(8,128)(2,1)}, bf16[2,656,1024]{2,1,0:T(8,128)(2,1)}, u32[]{:S(2)}, u32[]{:S(2)}) collective-permute-start(bf16[2,656,1024]{2,1,0:T(8,128)(2,1)} %dynamic-slice_bitcast_fusion.2), channel_id=1, source_target_pairs={{0,16},{16,0},{1,17},{17,1},{2,18},{18,2},{3,19},{19,3},{4,20},{20... | collective-permute-start | bytes 8060936 | tf_op jit(solution)/shard_map/ppermute | solution.py:62
  357.0 134.8 %collective-permute-start.23 = (bf16[2,256,5248]{2,1,0:T(8,128)(2,1)}, bf16[2,256,5248]{2,1,0:T(8,128)(2,1)}, u32[]{:S(2)}, u32[]{:S(2)}) collective-permute-start(bf16[2,256,5248]{2,1,0:T(8,128)(2,1)} %dynamic-slice_bitcast_fusion), channel_id=1, source_target_pairs={{0,16},{16,0},{1,17},{17,1},{2,18},{18,2},{3,19},{19,3},{4,20},{20... | collective-permute-start | bytes 16121864 | tf_op jit(solution)/shard_map/ppermute | solution.py:62
  361.9 19.8 %collective-permute-start.13 = (bf16[192,2048]{1,0:T(8,128)(2,1)S(1)}, bf16[192,2048]{1,0:T(8,128)(2,1)S(1)}, u32[]{:S(2)}, u32[]{:S(2)}) collective-permute-start(bf16[192,2048]{1,0:T(8,128)(2,1)S(1)} %add_convert_fusion.5), channel_id=1, source_target_pairs={{0,4},{4,8},{8,12},{12,14},{14,10},{10,6},{6,2},{2,0},{1,5},{5,9},... | collective-permute-start | bytes 2359304 | tf_op jit(solution)/shard_map/ppermute | solution.py:58
  365.9 19.5 %collective-permute-start.17 = (bf16[192,2048]{1,0:T(8,128)(2,1)S(1)}, bf16[192,2048]{1,0:T(8,128)(2,1)S(1)}, u32[]{:S(2)}, u32[]{:S(2)}) collective-permute-start(bf16[192,2048]{1,0:T(8,128)(2,1)S(1)} %add_convert_fusion.2), channel_id=1, source_target_pairs={{0,2},{4,0},{8,4},{12,8},{14,12},{10,14},{6,10},{2,6},{1,3},{5,1},... | collective-permute-start | bytes 2359304 | tf_op jit(solution)/shard_map/ppermute | solution.py:58
  385.5 20.8 %collective-permute-start.18 = (bf16[192,2048]{1,0:T(8,128)(2,1)S(1)}, bf16[192,2048]{1,0:T(8,128)(2,1)}, u32[]{:S(2)}, u32[]{:S(2)}) collective-permute-start(bf16[192,2048]{1,0:T(8,128)(2,1)S(1)} %add_convert_fusion.1), channel_id=1, source_target_pairs={{0,2},{4,0},{8,4},{12,8},{14,12},{10,14},{6,10},{2,6},{1,3},{5,1},... | collective-permute-start | bytes 2359304 | tf_op jit(solution)/shard_map/ppermute | solution.py:58
  432.6 53.0 %collective-permute-start.19 = (bf16[2,256,3072]{2,1,0:T(8,128)(2,1)}, bf16[2,256,3072]{2,1,0:T(8,128)(2,1)}, u32[]{:S(2)}, u32[]{:S(2)}) collective-permute-start(bf16[2,256,3072]{2,1,0:T(8,128)(2,1)} %dynamic-slice_bitcast_fusion.1), channel_id=1, source_target_pairs={{0,16},{16,0},{1,17},{17,1},{2,18},{18,2},{3,19},{19,3},{4,20},{20... | collective-permute-start | bytes 9437192 | tf_op jit(solution)/shard_map/ppermute | solution.py:62
  442.9 36.0 %collective-permute-start.26 = (bf16[656,1024]{1,0:T(8,128)(2,1)}, bf16[656,1024]{1,0:T(8,128)(2,1)}, u32[]{:S(2)}, u32[]{:S(2)}) collective-permute-start(bf16[656,1024]{1,0:T(8,128)(2,1)} %dynamic-slice_bitcast_fusion.5), channel_id=1, source_target_pairs={{0,1},{1,0},{2,3},{3,2},{4,5},{5,4},{6,7},{7,6},{8,9},{9,8},{10,11... | collective-permute-start | bytes 4030472 | tf_op jit(solution)/shard_map/ppermute | solution.py:62
  452.7 137.7 %reduce-scatter.11.cloned.1.call-start = ((), (), s32[]{:S(2)}) async-start(), calls=%async_computation.14 | async-start | bytes 1511424 | tf_op jit(solution)/shard_map/reduce_scatter | solution.py:110
  485.6 161.4 %reduce-scatter.5.cloned.1.call-start = ((), (), s32[]{:S(2)}) async-start(), calls=%async_computation.8 | async-start | bytes 1769472 | tf_op jit(solution)/shard_map/reduce_scatter | solution.py:110
  491.0 37.6 %collective-permute-start.20 = (bf16[256,3072]{1,0:T(8,128)(2,1)}, bf16[256,3072]{1,0:T(8,128)(2,1)}, u32[]{:S(2)}, u32[]{:S(2)}) collective-permute-start(bf16[256,3072]{1,0:T(8,128)(2,1)} %dynamic-slice_bitcast_fusion.4), channel_id=1, source_target_pairs={{0,1},{1,0},{2,3},{3,2},{4,5},{5,4},{6,7},{7,6},{8,9},{9,8},{10,11... | collective-permute-start | bytes 4718600 | tf_op jit(solution)/shard_map/ppermute | solution.py:62
  500.4 84.5 %collective-permute-start.24 = (bf16[256,5248]{1,0:T(8,128)(2,1)}, bf16[256,5248]{1,0:T(8,128)(2,1)}, u32[]{:S(2)}, u32[]{:S(2)}) collective-permute-start(bf16[256,5248]{1,0:T(8,128)(2,1)} %dynamic-slice_bitcast_fusion.3), channel_id=1, source_target_pairs={{0,1},{1,0},{2,3},{3,2},{4,5},{5,4},{6,7},{7,6},{8,9},{9,8},{10,11... | collective-permute-start | bytes 8060936 | tf_op jit(solution)/shard_map/ppermute | solution.py:62
  531.7 189.3 %reduce-scatter.9.cloned.1.call-start = ((), (), s32[]{:S(2)}) async-start(), calls=%async_computation.12 | async-start | bytes 3022848 | tf_op jit(solution)/shard_map/reduce_scatter | solution.py:110
  589.6 186.3 %all-gather.19.cloned.1.call-start = ((), (), s32[]{:S(2)}) async-start(), calls=%async_computation.11 | async-start | bytes 1114112 | tf_op jit(solution)/shard_map/all_gather | solution.py:111
  590.3 214.6 %all-gather.23.cloned.1.call-start = ((), (), s32[]{:S(2)}) async-start(), calls=%async_computation.15 | async-start | bytes 2854912 | tf_op jit(solution)/shard_map/all_gather | solution.py:111
  590.9 260.4 %all-gather.17.cloned.1.call-start = ((), (), s32[]{:S(2)}) async-start(), calls=%async_computation.9 | async-start | bytes 3342336 | tf_op jit(solution)/shard_map/all_gather | solution.py:111
  647.1 261.9 %all-gather.21.cloned.1.call-start = ((), (), s32[]{:S(2)}) async-start(), calls=%async_computation.13 | async-start | bytes 5709824 | tf_op jit(solution)/shard_map/all_gather | solution.py:111
  (146 other events, 796.1 us)
Sparse Core Ops, SparseCore 0:
  46.8 13.6 all-gather.8
  81.0 12.9 all-gather.14
  96.4 9.4 all-gather.10
  148.2 16.5 all-gather.12
  452.9 61.8 reduce-scatter.6
  518.4 60.6 reduce-scatter.10
  583.5 63.5 reduce-scatter.4
  651.1 69.8 reduce-scatter.8
  723.3 37.0 all-gather.18
  762.4 42.5 all-gather.22
  807.2 44.0 all-gather.16
  853.4 55.4 all-gather.20

commit v2 on v1

--- a/solution.py
+++ b/solution.py
@@ -62,10 +62,14 @@
     return lax.ppermute(value, axis, [(0, 1), (1, 0)])
 
 
-def fetch_rows(shard):
+def fetch_half(shard):
     part = shard.shape[0] // 2
     half = lax.dynamic_slice_in_dim(shard, lax.axis_index("dp") * part, part, 0)
-    return lax.all_gather(swap(half, "fsdp"), "dp", axis=0, tiled=True)
+    return swap(half, "fsdp")
+
+
+def trade_halves(half):
+    return lax.all_gather(half, "dp", axis=0, tiled=True)
 
 
 def halves_of(values, first):
@@ -99,17 +103,46 @@
     return lax.dynamic_index_in_dim(values, number, axis, keepdims=False)
 
 
-def reduce_rows(grads):
+def sum_cores(grads):
     rows, columns = grads.shape
-    core, shard = lax.axis_index("dp"), lax.axis_index("fsdp")
+    core = lax.axis_index("dp")
     quarters = grads.astype(jnp.bfloat16).reshape(2, 2, rows // 4, columns)
-    summed = add_low(pick(quarters, core, 1), swap(pick(quarters, 1 - core, 1), "dp"))
+    return add_low(pick(quarters, core, 1), swap(pick(quarters, 1 - core, 1), "dp"))
+
+
+def sum_shards(summed):
+    shard = lax.axis_index("fsdp")
     summed = add_low(pick(summed, shard, 0), swap(pick(summed, 1 - shard, 0), "fsdp"))
     if summed.shape[0] % (lax.axis_size("ctx") * 8):
         summed = summed.reshape(-1, 128)
-    piece = lax.psum_scatter(summed, "ctx", scatter_dimension=0, tiled=True)
+    return summed
+
+
+def sum_blocks(summed):
+    count = lax.axis_size("ctx")
+    if count > LONGEST_UNROLLED:
+        return lax.psum_scatter(summed, "ctx", scatter_dimension=0, tiled=True)
+    pieces = summed.reshape(count, summed.shape[0] // count, summed.shape[1])
+    index = lax.axis_index("ctx")
+    place = index // 2 + (index % 2) * (count - 1 - 2 * (index // 2))
+
+    def piece(steps):
+        there = (place + steps + count) % count
+        turned = there // (count // 2)
+        return pick(pieces, 2 * there + turned * (2 * count - 1 - 4 * there), 0)
+
+    forth, back = along_ring(piece(count // 2), 1), None
+    for step in range(count // 2 - 1, 0, -1):
+        forth = along_ring(add_low(piece(step), forth), 1)
+        behind = piece(-step)
+        back = along_ring(behind if back is None else add_low(behind, back), -1)
+    total = piece(0).astype(jnp.float32) + forth.astype(jnp.float32)
+    return (total + back.astype(jnp.float32)).astype(jnp.bfloat16)
+
+
+def share_rows(piece, columns):
     shared = lax.all_gather(piece, ("dp", "ctx"), axis=0, tiled=True)
-    return shared.reshape(rows // 2, columns).astype(jnp.float32)
+    return shared.reshape(-1, columns).astype(jnp.float32)
 
 
 def attend_block(queries, paired, state, scale):
@@ -161,10 +194,12 @@
     gains = jnp.stack([attn_gain, mlp_gain]).astype(jnp.float32)
     gains = join_halves(gains, swap(gains, "fsdp"), first)
     gain_att, gain_mlp = gains[0], gains[1]
-    other_qkv = fetch_rows(qkv_weight)
-    other_out = fetch_rows(out_weight)
-    other_in = fetch_rows(in_weight)
-    other_down = fetch_rows(down_weight)
+    other_qkv = trade_halves(fetch_half(qkv_weight))
+    half_out, half_in, half_down = (
+        fetch_half(out_weight),
+        fetch_half(in_weight),
+        fetch_half(down_weight),
+    )
     width = out_weight.shape[1]
     head_size = HEAD_DIM
     heads = width // head_size
@@ -204,6 +239,12 @@
             if step < cycle_size // 2:
                 after = along_ring(after, -1)
                 group.append(after)
+            if step == 3:
+                queries, state, half_out, half_in = lax.optimization_barrier(
+                    (queries, state, half_out, half_in)
+                )
+            if step == 4:
+                queries, state, half_down = lax.optimization_barrier((queries, state, half_down))
             state = attend_block(queries, as_heads(groups[-1]), state, scale)
             groups.append(group)
         best, total, summed = attend_block(queries, as_heads(groups[-1]), state, scale)
@@ -218,6 +259,11 @@
 
         state, paired = lax.fori_loop(0, cycle_size - 1, forward_turn, (state, local_pair))
         best, total, summed = attend_block(queries, as_heads([paired]), state, scale)
+    other_out, other_in, other_down = (
+        trade_halves(half_out),
+        trade_halves(half_in),
+        trade_halves(half_down),
+    )
     attended = summed / jnp.transpose(total)[:, :, None]
     log_total = best + jnp.log(total)
     attended_low = attended.reshape(row_count, width).astype(jnp.bfloat16)
@@ -245,6 +291,9 @@
     )
     delta = jnp.einsum("qhe,qhe->hq", grad_attended.astype(jnp.float32), attended)
 
+    sum_down, sum_in, sum_out = sum_cores(grad_down), sum_cores(grad_in), sum_cores(grad_wout)
+    if not unrolled:
+        sum_down, sum_in, sum_out = sum_shards(sum_down), sum_shards(sum_in), sum_shards(sum_out)
     grad_queries = jnp.zeros(shaped, jnp.float32)
 
     def back_pair(blocks, grad_queries):
@@ -256,6 +305,17 @@
     if unrolled:
         forth, back = None, None
         for step in range(cycle_size // 2, -1, -1):
+            if step == cycle_size // 2 - 1:
+                grad_attended, grad_queries, sum_down, sum_in, sum_out = lax.optimization_barrier(
+                    (grad_attended, grad_queries, sum_down, sum_in, sum_out)
+                )
+                sum_down = sum_shards(sum_down)
+                sum_in = sum_shards(sum_in)
+                sum_out = sum_shards(sum_out)
+            if step == 0:
+                grad_attended, grad_queries, sum_down, sum_in, sum_out = lax.optimization_barrier(
+                    (grad_attended, grad_queries, sum_down, sum_in, sum_out)
+                )
             grad_pair, grad_queries = back_pair(groups[step], grad_queries)
             if step == 0:
                 grad_pair = grad_pair + forth.astype(jnp.float32) + back.astype(jnp.float32)
@@ -295,17 +355,19 @@
     unused_att, pull_att = jax.vjp(layer_norm, inputs, gain_att)
     grad_inputs_att, grad_gain_att = pull_att(grad_normed)
     grad_inputs = grad_residual + grad_inputs_att
-    grad_gains = lax.psum(jnp.stack([grad_gain_att, grad_gain_mlp]), ("dp", "ctx", "fsdp"))
-    grad_gains, unused_half = halves_of(grad_gains, first)
+    extra = jnp.stack([grad_gain_att, grad_gain_mlp], 1)
+    extra = jnp.pad(extra, ((0, 0), (0, 126)))
+    joined = jnp.concatenate([grad_wqkv.astype(jnp.bfloat16), extra.astype(jnp.bfloat16)], 1)
+    summed_qkv = share_rows(sum_blocks(sum_shards(sum_cores(joined))), joined.shape[1])
     return (
         output.astype(jnp.bfloat16)[None],
         grad_inputs[None],
-        grad_gains[0],
-        reduce_rows(grad_wqkv),
-        reduce_rows(grad_wout),
-        grad_gains[1],
-        reduce_rows(grad_in),
-        reduce_rows(grad_down),
+        summed_qkv[:, 3 * width],
+        summed_qkv[:, : 3 * width],
+        share_rows(sum_blocks(sum_out), grad_wout.shape[1]),
+        summed_qkv[:, 3 * width + 1],
+        share_rows(sum_blocks(sum_in), grad_in.shape[1]),
+        share_rows(sum_blocks(sum_down), grad_down.shape[1]),
     )
 
 

time: 933 us -> 704 us (0.75)
  waiting for transfers between devices: 504 us -> 246 us
  blocking collectives: 39.8 us -> 0 us
  starting transfers between devices: 28.6 us -> 67.2 us
  other arithmetic: 101 us -> 116 us
  local copies, waits for them, and re-layouts: 120 us -> 130 us
    reduce_scatter x4 -> x0, waiting for transfers between devices: 130 us -> none  [reduce_rows(): piece = lax.psum_scatter(summed, 'ctx', scatter_dimension=0, tiled=True)]
    ppermute x13, waiting for transfers between devices: 200 us -> 95.7 us  [swap(): return lax.ppermute(value, axis, [(0, 1), (1, 0)])]
    all_gather x8, waiting for transfers between devices: 119 us -> 36.5 us  [the longest x4 36.5 us: share_rows(): shared = lax.all_gather(piece, ('dp', 'ctx'), axis=0, tiled=True)]
    ppermute x14 -> x42, waiting for transfers between devices: 53.5 us -> 113 us  [along_ring(): return lax.ppermute(value, 'ctx', ring_pairs(lax.axis_size('ctx'), steps))]
    psum x1 -> x0, blocking collectives: 39.8 us -> none  [local(): lax.psum(jnp.stack([grad_gain_att, grad_gain_mlp]), ('dp', 'ctx', 'fsdp'))]
    ppermute x14 -> x42, starting transfers between devices: 14.7 us -> 54.2 us  [along_ring(): return lax.ppermute(value, 'ctx', ring_pairs(lax.axis_size('ctx'), steps))]
    convert_element_type x8 -> x24, other arithmetic: 28.6 us -> 42.4 us  [add_low(): (left.astype(jnp.float32) + right.astype(jnp.float32)).astype(jnp.bfloat16)]
    dot_general x0 -> x3, matrix products: none -> 9.65 us  [back_block(): jnp.einsum('qhe,khe->hqk', queries, paired[0], preferred_element_type=jnp...]
  transfers between devices with their start and end apart: 39 -> 63, of which waited for: 18 -> 30; matrix products, arithmetic and copies ran while one was open for 27% -> 42% of each run, Pallas kernels for 0% -> 0%
where the time goes in v2:
time: 704 us; the launch traced here: 693 us
  waiting for transfers between devices  246 us (35%)
  local copies, waits for them, and re-layouts  130 us (18%)
  matrix products  118 us (17%)
  other arithmetic  116 us (16%)
  starting transfers between devices  67.2 us (10%)
  between operations  16.5 us (2%)
    ppermute x42, waiting for transfers between devices, along_ring(): return lax.ppermute(value, 'ctx', ring_pairs(lax.axis_size('ctx'), steps))  113 us
    ppermute x13, waiting for transfers between devices, swap(): return lax.ppermute(value, axis, [(0, 1), (1, 0)])  95.7 us
    ppermute x42, starting transfers between devices, along_ring(): return lax.ppermute(value, 'ctx', ring_pairs(lax.axis_size('ctx'), steps))  54.2 us
    convert_element_type x24, other arithmetic, add_low(): (left.astype(jnp.float32) + right.astype(jnp.float32)).astype(jnp.bfloat16)  42.4 us
    all_gather x4, waiting for transfers between devices, share_rows(): shared = lax.all_gather(piece, ('dp', 'ctx'), axis=0, tiled=True)  36.5 us
    unnamed x280, local copies, waits for them, and re-layouts  26.1 us
    squeeze x12, local copies, waits for them, and re-layouts, pick(): return lax.dynamic_index_in_dim(values, number, axis, keepdims=False)  20.4 us
    slice x6, local copies, waits for them, and re-layouts, local(): ahead = grad_pair[row_count:] + forth.astype(jnp.float32)  15.7 us
  transfers between devices with their start and end apart: 63, of which 30 were waited for; matrix products, arithmetic and copies ran while one was open for 42% of the time, Pallas kernels for 0%

profile of v2, /device:TPU:0, one launch (start us, length us, event | category | flops | bytes accessed | tf_op | source)
XLA Modules:
  0.0 693.1 jit_solution(3228661378448143937)
XLA Ops:
  15.2 32.3 %collective-permute-done.1 = bf16[256,3072]{1,0:T(8,128)(2,1)} collective-permute-done((bf16[256,3072]{1,0:T(8,128)(2,1)S(1)}, bf16[256,3072]{1,0:T(8,128)(2,1)}, u32[]{:S(2)}, u32[]{:S(2)}) %collective-permute-start.1) | collective-permute-done | bytes 1572896 | tf_op jit(solution)/shard_map/ppermute | solution.py:62
  100.4 5.4 collective-permute-done.3
  123.0 5.2 collective-permute-done.7
  160.7 7.2 %collective-permute-done.10 = bf16[192,2048]{1,0:T(8,128)(2,1)S(1)} collective-permute-done((bf16[192,2048]{1,0:T(8,128)(2,1)}, bf16[192,2048]{1,0:T(8,128)(2,1)S(1)}, u32[]{:S(2)}, u32[]{:S(2)}) %collective-permute-start.10) | collective-permute-done | bytes 786464 | tf_op jit(solution)/shard_map/ppermute | solution.py:58
  182.2 9.3 %collective-permute-done.11 = bf16[192,2048]{1,0:T(8,128)(2,1)} collective-permute-done((bf16[192,2048]{1,0:T(8,128)(2,1)}, bf16[192,2048]{1,0:T(8,128)(2,1)}, u32[]{:S(2)}, u32[]{:S(2)}) %collective-permute-start.11) | collective-permute-done | bytes 786464 | tf_op jit(solution)/shard_map/ppermute | solution.py:58
  212.1 5.8 fusion.196
  221.7 5.3 convolution_add_fusion
  227.1 4.8 fusion.133
  239.4 5.2 convolution_convert_fusion
  277.9 5.8 fusion.5
  283.8 7.9 %fusion.1 = bf16[2,256,5248]{2,1,0:T(8,128)(2,1)} fusion(bf16[2,256,5248]{2,1,0:T(8,128)(2,1)} %collective-permute-done.13, bf16[2,2,256,5248]{3,2,1,0:T(8,128)(2,1)} %bitcast.430, s32[]{:T(128)S(6)} %select_n.339), kind=kLoop, calls=%fused_computation.4 | loop fusion | flops 10747904 | bytes 16121860 | tf_op jit(solution)/shard_map/convert_element_type | solution.py:99
  293.8 4.5 multiply_convert_fusion
  357.7 8.1 %collective-permute-done.19 = bf16[192,2048]{1,0:T(8,128)(2,1)S(1)} collective-permute-done((bf16[192,2048]{1,0:T(8,128)(2,1)S(1)}, bf16[192,2048]{1,0:T(8,128)(2,1)S(1)}, u32[]{:S(2)}, u32[]{:S(2)}) %collective-permute-start.19) | collective-permute-done | bytes 786464 | tf_op jit(solution)/shard_map/ppermute | solution.py:58
  368.0 5.7 collective-permute-done.23
  376.1 7.3 %collective-permute-done.20 = bf16[192,2048]{1,0:T(8,128)(2,1)S(1)} collective-permute-done((bf16[192,2048]{1,0:T(8,128)(2,1)S(1)}, bf16[192,2048]{1,0:T(8,128)(2,1)S(1)}, u32[]{:S(2)}, u32[]{:S(2)}) %collective-permute-start.20) | collective-permute-done | bytes 786464 | tf_op jit(solution)/shard_map/ppermute | solution.py:58
  387.5 26.0 %collective-permute-done.17 = bf16[256,1024]{1,0:T(8,128)(2,1)} collective-permute-done((bf16[256,1024]{1,0:T(8,128)(2,1)}, bf16[256,1024]{1,0:T(8,128)(2,1)}, u32[]{:S(2)}, u32[]{:S(2)}) %collective-permute-start.17) | collective-permute-done | bytes 524320 | tf_op jit(solution)/shard_map/ppermute | solution.py:62
  426.2 4.8 fusion.4
  440.6 4.6 convolution_convert_fusion.2
  483.3 5.4 collective-permute-done.50
  498.2 6.1 fusion.2
  519.1 4.6 collective-permute-done.44
  532.4 34.6 %collective-permute-done.26 = bf16[256,3200]{1,0:T(8,128)(2,1)S(1)} collective-permute-done((bf16[256,3200]{1,0:T(8,128)(2,1)S(1)}, bf16[256,3200]{1,0:T(8,128)(2,1)S(1)}, u32[]{:S(2)}, u32[]{:S(2)}) %collective-permute-start.26) | collective-permute-done | bytes 1638432 | tf_op jit(solution)/shard_map/ppermute | solution.py:62
  569.0 4.5 collective-permute-done.27
  576.1 9.6 %collective-permute-done.28 = bf16[32,3200]{1,0:T(8,128)(2,1)S(1)} collective-permute-done((bf16[32,3200]{1,0:T(8,128)(2,1)S(1)}, bf16[32,3200]{1,0:T(8,128)(2,1)S(1)}, u32[]{:S(2)}, u32[]{:S(2)}) %collective-permute-start.28) | collective-permute-done | bytes 204832 | tf_op jit(solution)/shard_map/ppermute | solution.py:58
  585.7 4.9 collective-permute-start.29
  590.7 4.7 collective-permute-done.29
  595.5 4.6 collective-permute-start.32
  600.1 7.3 %collective-permute-done.32 = bf16[32,3200]{1,0:T(8,128)(2,1)S(1)} collective-permute-done((bf16[32,3200]{1,0:T(8,128)(2,1)S(1)}, bf16[32,3200]{1,0:T(8,128)(2,1)S(1)}, u32[]{:S(2)}, u32[]{:S(2)}) %collective-permute-start.32) | collective-permute-done | bytes 204832 | tf_op jit(solution)/shard_map/ppermute | solution.py:58
  610.0 8.9 %collective-permute-done.33 = bf16[32,3200]{1,0:T(8,128)(2,1)S(1)} collective-permute-done((bf16[32,3200]{1,0:T(8,128)(2,1)S(1)}, bf16[32,3200]{1,0:T(8,128)(2,1)S(1)}, u32[]{:S(2)}, u32[]{:S(2)}) %collective-permute-start.33) | collective-permute-done | bytes 204832 | tf_op jit(solution)/shard_map/ppermute | solution.py:58
  629.5 5.6 reshape.316
  635.1 7.4 %convert_element_type.742 = f32[512,5248]{1,0:T(8,128)} convert(bf16[512,5248]{1,0:T(8,128)(2,1)} %all-gather.21.cloned.1.call-done) | non-fusion elementwise | flops 2686976 | bytes 16121856 | tf_op jit(solution)/shard_map/convert_element_type | solution.py:145
  642.5 36.5 %all-gather.17.cloned.1.call-done = bf16[512,3200]{1,0:T(8,128)(2,1)} async-done(((bf16[32,3200]{1,0:T(8,128)(2,1)}), bf16[512,3200]{1,0:T(8,128)(2,1)}) %all-gather.17.cloned.1.call-update) | async-done | bytes 3276816 | tf_op jit(solution)/shard_map/all_gather | solution.py:144
  (597 shorter events, 376.2 us)
Async XLA Ops:
  7.2 59.6 %all-gather.9.cloned.1.call-start = ((), (), s32[]{:S(2)}) async-start(), calls=%async_computation | async-start | bytes 4718592 | tf_op jit(solution)/shard_map/all_gather | solution.py:72
  9.2 38.3 %collective-permute-start.1 = (bf16[256,3072]{1,0:T(8,128)(2,1)S(1)}, bf16[256,3072]{1,0:T(8,128)(2,1)}, u32[]{:S(2)}, u32[]{:S(2)}) collective-permute-start(bf16[256,3072]{1,0:T(8,128)(2,1)S(1)} %constant_dynamic-slice_fusion.3), channel_id=1, source_target_pairs={{0,1},{1,0},{2,3},{3,2},{4,5},{5,4},{6,7},{7,6},{8,9},{9,8},{10,11... | collective-permute-start | bytes 4718600 | tf_op jit(solution)/shard_map/ppermute | solution.py:62
  12.2 50.2 %collective-permute-start = (f32[2,512]{1,0:T(2,128)S(1)}, f32[2,512]{1,0:T(2,128)S(1)}, u32[]{:S(2)}, u32[]{:S(2)}) collective-permute-start(f32[2,512]{1,0:T(2,128)S(1)} %maximum_convert_fusion), channel_id=1, source_target_pairs={{0,1},{1,0},{2,3},{3,2},{4,5},{5,4},{6,7},{7,6},{8,9},{9,8},{10,11... | collective-permute-start | bytes 12296 | tf_op jit(solution)/shard_map/ppermute | solution.py:62
  13.2 109.6 %collective-permute-start.4 = (bf16[256,1024]{1,0:T(8,128)(2,1)}, bf16[256,1024]{1,0:T(8,128)(2,1)}, u32[]{:S(2)}, u32[]{:S(2)}) collective-permute-start(bf16[256,1024]{1,0:T(8,128)(2,1)} %constant_dynamic-slice_fusion.2), channel_id=1, source_target_pairs={{0,1},{1,0},{2,3},{3,2},{4,5},{5,4},{6,7},{7,6},{8,9},{9,8},{10,11... | collective-permute-start | bytes 1572872 | tf_op jit(solution)/shard_map/ppermute | solution.py:62
  47.5 160.7 %all-gather.11.cloned.1.call-start = ((), (), s32[]{:S(2)}) async-start(), calls=%async_computation.1 | async-start | bytes 1572864 | tf_op jit(solution)/shard_map/all_gather | solution.py:72
  51.0 71.7 %collective-permute-start.5 = (bf16[256,5248]{1,0:T(8,128)(2,1)}, bf16[256,5248]{1,0:T(8,128)(2,1)}, u32[]{:S(2)}, u32[]{:S(2)}) collective-permute-start(bf16[256,5248]{1,0:T(8,128)(2,1)} %constant_dynamic-slice_fusion.1), channel_id=1, source_target_pairs={{0,1},{1,0},{2,3},{3,2},{4,5},{5,4},{6,7},{7,6},{8,9},{9,8},{10,11... | collective-permute-start | bytes 8060936 | tf_op jit(solution)/shard_map/ppermute | solution.py:62
  55.6 88.8 %collective-permute-start.8 = (bf16[656,1024]{1,0:T(8,128)(2,1)}, bf16[656,1024]{1,0:T(8,128)(2,1)}, u32[]{:S(2)}, u32[]{:S(2)}) collective-permute-start(bf16[656,1024]{1,0:T(8,128)(2,1)} %constant_dynamic-slice_fusion), channel_id=1, source_target_pairs={{0,1},{1,0},{2,3},{3,2},{4,5},{5,4},{6,7},{7,6},{8,9},{9,8},{10,11... | collective-permute-start | bytes 4030472 | tf_op jit(solution)/shard_map/ppermute | solution.py:62
  88.2 17.7 %collective-permute-start.3 = (bf16[192,2048]{1,0:T(8,128)(2,1)}, bf16[192,2048]{1,0:T(8,128)(2,1)}, u32[]{:S(2)}, u32[]{:S(2)}) collective-permute-start(bf16[192,2048]{1,0:T(8,128)(2,1)} %pad_maximum_fusion.7), channel_id=1, source_target_pairs={{0,2},{4,0},{8,4},{12,8},{14,12},{10,14},{6,10},{2,6},{1,3},{5,1},... | collective-permute-start | bytes 2359304 | tf_op jit(solution)/shard_map/ppermute | solution.py:58
  122.8 95.0 %all-gather.15.cloned.1.call-start = ((), (), s32[]{:S(2)}) async-start(), calls=%async_computation.3 | async-start | bytes 4030464 | tf_op jit(solution)/shard_map/all_gather | solution.py:72
  144.4 77.3 %all-gather.13.cloned.1.call-start = ((), (), s32[]{:S(2)}) async-start(), calls=%async_computation.2 | async-start | bytes 8060928 | tf_op jit(solution)/shard_map/all_gather | solution.py:72
  148.8 477.8 %all-gather.19.cloned.1.call-start = ((), (), s32[]{:S(2)}) async-start(), calls=%async_computation.5 | async-start | bytes 1114112 | tf_op jit(solution)/shard_map/all_gather | solution.py:144
  148.9 19.0 %collective-permute-start.10 = (bf16[192,2048]{1,0:T(8,128)(2,1)}, bf16[192,2048]{1,0:T(8,128)(2,1)S(1)}, u32[]{:S(2)}, u32[]{:S(2)}) collective-permute-start(bf16[192,2048]{1,0:T(8,128)(2,1)} %collective-permute-done.7), channel_id=1, source_target_pairs={{0,2},{4,0},{8,4},{12,8},{14,12},{10,14},{6,10},{2,6},{1,3},{5,1},... | collective-permute-start | bytes 2359304 | tf_op jit(solution)/shard_map/ppermute | solution.py:58
  150.7 18.3 %collective-permute-start.9 = (bf16[192,2048]{1,0:T(8,128)(2,1)}, bf16[192,2048]{1,0:T(8,128)(2,1)S(1)}, u32[]{:S(2)}, u32[]{:S(2)}) collective-permute-start(bf16[192,2048]{1,0:T(8,128)(2,1)} %collective-permute-done.6), channel_id=1, source_target_pairs={{0,4},{4,8},{8,12},{12,14},{14,10},{10,6},{6,2},{2,0},{1,5},{5,9},... | collective-permute-start | bytes 2359304 | tf_op jit(solution)/shard_map/ppermute | solution.py:58
  174.2 17.3 %collective-permute-start.11 = (bf16[192,2048]{1,0:T(8,128)(2,1)}, bf16[192,2048]{1,0:T(8,128)(2,1)}, u32[]{:S(2)}, u32[]{:S(2)}) collective-permute-start(bf16[192,2048]{1,0:T(8,128)(2,1)} %copy-done.91), channel_id=1, source_target_pairs={{0,4},{4,8},{8,12},{12,14},{14,10},{10,6},{6,2},{2,0},{1,5},{5,9},... | collective-permute-start | bytes 2359304 | tf_op jit(solution)/shard_map/ppermute | solution.py:58
  250.4 33.3 %collective-permute-start.13 = (bf16[2,256,5248]{2,1,0:T(8,128)(2,1)}, bf16[2,256,5248]{2,1,0:T(8,128)(2,1)}, u32[]{:S(2)}, u32[]{:S(2)}) collective-permute-start(bf16[2,256,5248]{2,1,0:T(8,128)(2,1)} %dynamic-slice_bitcast_fusion), channel_id=1, source_target_pairs={{0,16},{16,0},{1,17},{17,1},{2,18},{18,2},{3,19},{19,3},{4,20},{20... | collective-permute-start | bytes 16121864 | tf_op jit(solution)/shard_map/ppermute | solution.py:62
  254.1 23.9 %collective-permute-start.12 = (bf16[2,656,1024]{2,1,0:T(8,128)(2,1)}, bf16[2,656,1024]{2,1,0:T(8,128)(2,1)}, u32[]{:S(2)}, u32[]{:S(2)}) collective-permute-start(bf16[2,656,1024]{2,1,0:T(8,128)(2,1)} %dynamic-slice_bitcast_fusion.3), channel_id=1, source_target_pairs={{0,16},{16,0},{1,17},{17,1},{2,18},{18,2},{3,19},{19,3},{4,20},{20... | collective-permute-start | bytes 8060936 | tf_op jit(solution)/shard_map/ppermute | solution.py:62
  271.1 74.7 %collective-permute-start.18 = (bf16[192,2048]{1,0:T(8,128)(2,1)}, bf16[192,2048]{1,0:T(8,128)(2,1)}, u32[]{:S(2)}, u32[]{:S(2)}) collective-permute-start(bf16[192,2048]{1,0:T(8,128)(2,1)} %copy.156), channel_id=1, source_target_pairs={{0,4},{4,8},{8,12},{12,14},{14,10},{10,6},{6,2},{2,0},{1,5},{5,9},... | collective-permute-start | bytes 2359304 | tf_op jit(solution)/shard_map/ppermute | solution.py:58
  313.2 102.4 %collective-permute-start.15 = (bf16[656,1024]{1,0:T(8,128)(2,1)}, bf16[656,1024]{1,0:T(8,128)(2,1)}, u32[]{:S(2)}, u32[]{:S(2)}) collective-permute-start(bf16[656,1024]{1,0:T(8,128)(2,1)} %dynamic-slice_bitcast_fusion.5), channel_id=1, source_target_pairs={{0,1},{1,0},{2,3},{3,2},{4,5},{5,4},{6,7},{7,6},{8,9},{9,8},{10,11... | collective-permute-start | bytes 4030472 | tf_op jit(solution)/shard_map/ppermute | solution.py:62
  316.2 110.1 %collective-permute-start.16 = (bf16[256,5248]{1,0:T(8,128)(2,1)}, bf16[256,5248]{1,0:T(8,128)(2,1)}, u32[]{:S(2)}, u32[]{:S(2)}) collective-permute-start(bf16[256,5248]{1,0:T(8,128)(2,1)} %dynamic-slice_bitcast_fusion.2), channel_id=1, source_target_pairs={{0,1},{1,0},{2,3},{3,2},{4,5},{5,4},{6,7},{7,6},{8,9},{9,8},{10,11... | collective-permute-start | bytes 8060936 | tf_op jit(solution)/shard_map/ppermute | solution.py:62
  317.8 95.7 %collective-permute-start.17 = (bf16[256,1024]{1,0:T(8,128)(2,1)}, bf16[256,1024]{1,0:T(8,128)(2,1)}, u32[]{:S(2)}, u32[]{:S(2)}) collective-permute-start(bf16[256,1024]{1,0:T(8,128)(2,1)} %dynamic-slice_bitcast_fusion.7), channel_id=1, source_target_pairs={{0,1},{1,0},{2,3},{3,2},{4,5},{5,4},{6,7},{7,6},{8,9},{9,8},{10,11... | collective-permute-start | bytes 1572872 | tf_op jit(solution)/shard_map/ppermute | solution.py:62
  336.0 18.7 %collective-permute-start.22 = (bf16[192,2048]{1,0:T(8,128)(2,1)}, bf16[192,2048]{1,0:T(8,128)(2,1)}, u32[]{:S(2)}, u32[]{:S(2)}) collective-permute-start(bf16[192,2048]{1,0:T(8,128)(2,1)} %copy.161), channel_id=1, source_target_pairs={{0,2},{4,0},{8,4},{12,8},{14,12},{10,14},{6,10},{2,6},{1,3},{5,1},... | collective-permute-start | bytes 2359304 | tf_op jit(solution)/shard_map/ppermute | solution.py:58
  347.8 18.1 %collective-permute-start.19 = (bf16[192,2048]{1,0:T(8,128)(2,1)S(1)}, bf16[192,2048]{1,0:T(8,128)(2,1)S(1)}, u32[]{:S(2)}, u32[]{:S(2)}) collective-permute-start(bf16[192,2048]{1,0:T(8,128)(2,1)S(1)} %add_convert_fusion.5), channel_id=1, source_target_pairs={{0,4},{4,8},{8,12},{12,14},{14,10},{10,6},{6,2},{2,0},{1,5},{5,9},... | collective-permute-start | bytes 2359304 | tf_op jit(solution)/shard_map/ppermute | solution.py:58
  356.2 17.5 %collective-permute-start.23 = (bf16[192,2048]{1,0:T(8,128)(2,1)S(1)}, bf16[192,2048]{1,0:T(8,128)(2,1)S(1)}, u32[]{:S(2)}, u32[]{:S(2)}) collective-permute-start(bf16[192,2048]{1,0:T(8,128)(2,1)S(1)} %add_convert_fusion.2), channel_id=1, source_target_pairs={{0,2},{4,0},{8,4},{12,8},{14,12},{10,14},{6,10},{2,6},{1,3},{5,1},... | collective-permute-start | bytes 2359304 | tf_op jit(solution)/shard_map/ppermute | solution.py:58
  366.1 17.4 %collective-permute-start.20 = (bf16[192,2048]{1,0:T(8,128)(2,1)S(1)}, bf16[192,2048]{1,0:T(8,128)(2,1)S(1)}, u32[]{:S(2)}, u32[]{:S(2)}) collective-permute-start(bf16[192,2048]{1,0:T(8,128)(2,1)S(1)} %add_convert_fusion.4), channel_id=1, source_target_pairs={{0,4},{4,8},{8,12},{12,14},{14,10},{10,6},{6,2},{2,0},{1,5},{5,9},... | collective-permute-start | bytes 2359304 | tf_op jit(solution)/shard_map/ppermute | solution.py:58
  374.8 47.0 %collective-permute-start.24 = (bf16[192,2048]{1,0:T(8,128)(2,1)}, bf16[192,2048]{1,0:T(8,128)(2,1)}, u32[]{:S(2)}, u32[]{:S(2)}) collective-permute-start(bf16[192,2048]{1,0:T(8,128)(2,1)} %add_convert_fusion.1), channel_id=1, source_target_pairs={{0,2},{4,0},{8,4},{12,8},{14,12},{10,14},{6,10},{2,6},{1,3},{5,1},... | collective-permute-start | bytes 2359304 | tf_op jit(solution)/shard_map/ppermute | solution.py:58
  384.6 39.4 %collective-permute-start.21 = (bf16[192,2048]{1,0:T(8,128)(2,1)}, bf16[192,2048]{1,0:T(8,128)(2,1)}, u32[]{:S(2)}, u32[]{:S(2)}) collective-permute-start(bf16[192,2048]{1,0:T(8,128)(2,1)} %add_convert_fusion.3), channel_id=1, source_target_pairs={{0,4},{4,8},{8,12},{12,14},{14,10},{10,6},{6,2},{2,0},{1,5},{5,9},... | collective-permute-start | bytes 2359304 | tf_op jit(solution)/shard_map/ppermute | solution.py:58
  459.4 46.7 %collective-permute-start.45 = (bf16[32,5248]{1,0:T(8,128)(2,1)}, bf16[32,5248]{1,0:T(8,128)(2,1)}, u32[]{:S(2)}, u32[]{:S(2)}) collective-permute-start(bf16[32,5248]{1,0:T(8,128)(2,1)} %get-tuple-element.81), channel_id=1, source_target_pairs={{0,2},{4,0},{8,4},{12,8},{14,12},{10,14},{6,10},{2,6},{1,3},{5,1},... | collective-permute-start | bytes 1007624 | tf_op jit(solution)/shard_map/ppermute | solution.py:58
  465.5 17.8 %collective-permute-start.52 = (bf16[656,128]{1,0:T(8,128)(2,1)}, bf16[656,128]{1,0:T(8,128)(2,1)}, u32[]{:S(2)}, u32[]{:S(2)}) collective-permute-start(bf16[656,128]{1,0:T(8,128)(2,1)} %get-tuple-element.91), channel_id=1, source_target_pairs={{0,2},{4,0},{8,4},{12,8},{14,12},{10,14},{6,10},{2,6},{1,3},{5,1},... | collective-permute-start | bytes 503816 | tf_op jit(solution)/shard_map/ppermute | solution.py:58
  483.2 146.3 %all-gather.23.cloned.1.call-start = ((), (), s32[]{:S(2)}) async-start(), calls=%async_computation.7 | async-start | bytes 2854912 | tf_op jit(solution)/shard_map/all_gather | solution.py:144
  506.0 129.1 %all-gather.21.cloned.1.call-start = ((), (), s32[]{:S(2)}) async-start(), calls=%async_computation.6 | async-start | bytes 5709824 | tf_op jit(solution)/shard_map/all_gather | solution.py:144
  527.0 152.0 %all-gather.17.cloned.1.call-start = ((), (), s32[]{:S(2)}) async-start(), calls=%async_computation.4 | async-start | bytes 3481600 | tf_op jit(solution)/shard_map/all_gather | solution.py:144
  531.0 36.1 %collective-permute-start.26 = (bf16[256,3200]{1,0:T(8,128)(2,1)S(1)}, bf16[256,3200]{1,0:T(8,128)(2,1)S(1)}, u32[]{:S(2)}, u32[]{:S(2)}) collective-permute-start(bf16[256,3200]{1,0:T(8,128)(2,1)S(1)} %dynamic-slice_bitcast_fusion.4), channel_id=1, source_target_pairs={{0,1},{1,0},{2,3},{3,2},{4,5},{5,4},{6,7},{7,6},{8,9},{9,8},{10,11... | collective-permute-start | bytes 4915208 | tf_op jit(solution)/shard_map/ppermute | solution.py:62
  (170 other events, 1029.3 us)
Sparse Core Ops, SparseCore 0:
  47.6 13.9 all-gather.8
  122.9 9.3 all-gather.10
  144.5 12.9 all-gather.14
  158.9 16.5 all-gather.12
  483.4 36.9 all-gather.18
  522.4 43.1 all-gather.22
  568.4 60.3 all-gather.20
  630.9 48.0 all-gather.16

commit v3 on v2

--- a/solution.py
+++ b/solution.py
@@ -229,7 +229,7 @@
         jnp.zeros((heads, row_count), jnp.float32),
         jnp.zeros(shaped, jnp.float32),
     )
-    unrolled = cycle_size <= LONGEST_UNROLLED
+    unrolled = 4 <= cycle_size <= LONGEST_UNROLLED
     groups = [[local_pair]]
     if unrolled:
         before, after = local_pair, local_pair
@@ -310,11 +310,15 @@
                     (grad_attended, grad_queries, sum_down, sum_in, sum_out)
                 )
                 sum_down = sum_shards(sum_down)
+                sum_out = sum_shards(sum_out)
+            if step == cycle_size // 2 - 2:
+                grad_attended, grad_queries, sum_in = lax.optimization_barrier(
+                    (grad_attended, grad_queries, sum_in)
+                )
                 sum_in = sum_shards(sum_in)
-                sum_out = sum_shards(sum_out)
             if step == 0:
-                grad_attended, grad_queries, sum_down, sum_in, sum_out = lax.optimization_barrier(
-                    (grad_attended, grad_queries, sum_down, sum_in, sum_out)
+                grad_attended, grad_queries, sum_down, sum_out = lax.optimization_barrier(
+                    (grad_attended, grad_queries, sum_down, sum_out)
                 )
             grad_pair, grad_queries = back_pair(groups[step], grad_queries)
             if step == 0:
@@ -358,7 +362,8 @@
     extra = jnp.stack([grad_gain_att, grad_gain_mlp], 1)
     extra = jnp.pad(extra, ((0, 0), (0, 126)))
     joined = jnp.concatenate([grad_wqkv.astype(jnp.bfloat16), extra.astype(jnp.bfloat16)], 1)
-    summed_qkv = share_rows(sum_blocks(sum_shards(sum_cores(joined))), joined.shape[1])
+    sum_qkv, sum_in = lax.optimization_barrier((sum_cores(joined), sum_in))
+    summed_qkv = share_rows(sum_blocks(sum_shards(sum_qkv)), joined.shape[1])
     return (
         output.astype(jnp.bfloat16)[None],
         grad_inputs[None],

time: 704 us -> 694 us (0.986)
  waiting for transfers between devices: 246 us -> 222 us
  other arithmetic: 116 us -> 129 us
    ppermute x13, waiting for transfers between devices: 95.7 us -> 48 us  [swap(): return lax.ppermute(value, axis, [(0, 1), (1, 0)])]
    all_gather x4, waiting for transfers between devices: 36.5 us -> 57.3 us  [share_rows(): shared = lax.all_gather(piece, ('dp', 'ctx'), axis=0, tiled=True)]
    unnamed x280 -> x288, local copies, waits for them, and re-layouts: 26.1 us -> 30 us
  transfers between devices with their start and end apart: 63 -> 63, of which waited for: 30 -> 32; matrix products, arithmetic and copies ran while one was open for 42% -> 48% of each run, Pallas kernels for 0% -> 0%
where the time goes in v3:
time: 694 us; the launch traced here: 683 us
  waiting for transfers between devices  222 us (32%)
  local copies, waits for them, and re-layouts  135 us (19%)
  other arithmetic  129 us (19%)
  matrix products  120 us (17%)
  starting transfers between devices  61.6 us (9%)
  between operations  16.3 us (2%)
    ppermute x42, waiting for transfers between devices, along_ring(): return lax.ppermute(value, 'ctx', ring_pairs(lax.axis_size('ctx'), steps))  116 us
    all_gather x4, waiting for transfers between devices, share_rows(): shared = lax.all_gather(piece, ('dp', 'ctx'), axis=0, tiled=True)  57.3 us
    ppermute x42, starting transfers between devices, along_ring(): return lax.ppermute(value, 'ctx', ring_pairs(lax.axis_size('ctx'), steps))  48.4 us
    ppermute x13, waiting for transfers between devices, swap(): return lax.ppermute(value, axis, [(0, 1), (1, 0)])  48 us
    convert_element_type x24, other arithmetic, add_low(): (left.astype(jnp.float32) + right.astype(jnp.float32)).astype(jnp.bfloat16)  43.7 us
    unnamed x288, local copies, waits for them, and re-layouts  30 us
    squeeze x12, local copies, waits for them, and re-layouts, pick(): return lax.dynamic_index_in_dim(values, number, axis, keepdims=False)  19.5 us
    slice x6, local copies, waits for them, and re-layouts, local(): ahead = grad_pair[row_count:] + forth.astype(jnp.float32)  18 us
  transfers between devices with their start and end apart: 63, of which 32 were waited for; matrix products, arithmetic and copies ran while one was open for 48% of the time, Pallas kernels for 0%

profile of v3, /device:TPU:0, one launch (start us, length us, event | category | flops | bytes accessed | tf_op | source)
XLA Modules:
  0.0 683.3 jit_solution(6415758746271005486)
XLA Ops:
  15.1 32.4 %collective-permute-done.1 = bf16[256,3072]{1,0:T(8,128)(2,1)} collective-permute-done((bf16[256,3072]{1,0:T(8,128)(2,1)S(1)}, bf16[256,3072]{1,0:T(8,128)(2,1)}, u32[]{:S(2)}, u32[]{:S(2)}) %collective-permute-start.1) | collective-permute-done | bytes 1572896 | tf_op jit(solution)/shard_map/ppermute | solution.py:62
  100.5 5.5 collective-permute-done.3
  123.3 4.9 collective-permute-done.7
  144.5 4.0 fusion.188
  160.1 7.5 %collective-permute-done.10 = bf16[192,2048]{1,0:T(8,128)(2,1)S(1)} collective-permute-done((bf16[192,2048]{1,0:T(8,128)(2,1)}, bf16[192,2048]{1,0:T(8,128)(2,1)S(1)}, u32[]{:S(2)}, u32[]{:S(2)}) %collective-permute-start.10) | collective-permute-done | bytes 786464 | tf_op jit(solution)/shard_map/ppermute | solution.py:58
  181.8 9.4 %collective-permute-done.11 = bf16[192,2048]{1,0:T(8,128)(2,1)} collective-permute-done((bf16[192,2048]{1,0:T(8,128)(2,1)}, bf16[192,2048]{1,0:T(8,128)(2,1)}, u32[]{:S(2)}, u32[]{:S(2)}) %collective-permute-start.11) | collective-permute-done | bytes 786464 | tf_op jit(solution)/shard_map/ppermute | solution.py:58
  211.7 5.8 fusion.198
  221.4 5.3 convolution_add_fusion
  226.7 4.8 fusion.134
  233.3 4.0 convolution_convert_fusion.1
  237.8 5.5 convolution_convert_fusion
  278.4 4.0 fusion.5
  282.6 8.7 %fusion.1 = bf16[2,256,5248]{2,1,0:T(8,128)(2,1)} fusion(bf16[2,256,5248]{2,1,0:T(8,128)(2,1)} %collective-permute-done.13, bf16[2,2,256,5248]{3,2,1,0:T(8,128)(2,1)} %bitcast.436, s32[]{:T(128)S(6)} %select_n.339), kind=kLoop, calls=%fused_computation.4 | loop fusion | flops 10747904 | bytes 16121860 | tf_op jit(solution)/shard_map/convert_element_type | solution.py:99
  295.2 4.0 multiply_convert_fusion
  333.6 5.1 fusion.253
  382.5 4.7 collective-permute-done.22
  398.1 7.9 %collective-permute-done.23 = bf16[192,2048]{1,0:T(8,128)(2,1)} collective-permute-done((bf16[192,2048]{1,0:T(8,128)(2,1)S(1)}, bf16[192,2048]{1,0:T(8,128)(2,1)}, u32[]{:S(2)}, u32[]{:S(2)}) %collective-permute-start.23) | collective-permute-done | bytes 786464 | tf_op jit(solution)/shard_map/ppermute | solution.py:58
  419.7 4.6 convolution_convert_fusion.2
  442.7 4.9 fusion.4
  468.0 4.7 collective-permute-done.50
  476.2 12.9 %collective-permute-done.26 = bf16[256,3200]{1,0:T(8,128)(2,1)} collective-permute-done((bf16[256,3200]{1,0:T(8,128)(2,1)}, bf16[256,3200]{1,0:T(8,128)(2,1)}, u32[]{:S(2)}, u32[]{:S(2)}) %collective-permute-start.26) | collective-permute-done | bytes 1638432 | tf_op jit(solution)/shard_map/ppermute | solution.py:62
  495.3 5.6 collective-permute-done.27
  509.4 5.2 collective-permute-done.29
  521.7 4.5 collective-permute-done.32
  538.5 11.4 %collective-permute-done.42 = bf16[32,5248]{1,0:T(8,128)(2,1)} collective-permute-done((bf16[32,5248]{1,0:T(8,128)(2,1)}, bf16[32,5248]{1,0:T(8,128)(2,1)}, u32[]{:S(2)}, u32[]{:S(2)}) %collective-permute-start.42) | collective-permute-done | bytes 335904 | tf_op jit(solution)/shard_map/ppermute | solution.py:58
  554.3 8.5 %collective-permute-done.43 = bf16[32,5248]{1,0:T(8,128)(2,1)S(1)} collective-permute-done((bf16[32,5248]{1,0:T(8,128)(2,1)S(1)}, bf16[32,5248]{1,0:T(8,128)(2,1)S(1)}, u32[]{:S(2)}, u32[]{:S(2)}) %collective-permute-start.43) | collective-permute-done | bytes 335904 | tf_op jit(solution)/shard_map/ppermute | solution.py:58
  568.0 7.6 %collective-permute-done.46 = bf16[32,5248]{1,0:T(8,128)(2,1)S(1)} collective-permute-done((bf16[32,5248]{1,0:T(8,128)(2,1)S(1)}, bf16[32,5248]{1,0:T(8,128)(2,1)S(1)}, u32[]{:S(2)}, u32[]{:S(2)}) %collective-permute-start.46) | collective-permute-done | bytes 335904 | tf_op jit(solution)/shard_map/ppermute | solution.py:58
  579.2 7.4 %collective-permute-done.47 = bf16[32,5248]{1,0:T(8,128)(2,1)S(1)} collective-permute-done((bf16[32,5248]{1,0:T(8,128)(2,1)S(1)}, bf16[32,5248]{1,0:T(8,128)(2,1)S(1)}, u32[]{:S(2)}, u32[]{:S(2)}) %collective-permute-start.47) | collective-permute-done | bytes 335904 | tf_op jit(solution)/shard_map/ppermute | solution.py:58
  598.3 5.6 reshape.316
  603.9 6.3 all-gather.17.cloned.1.call-done
  617.5 51.1 %all-gather.21.cloned.1.call-done = bf16[512,5248]{1,0:T(8,128)(2,1)} async-done(((bf16[32,5248]{1,0:T(8,128)(2,1)}), bf16[512,5248]{1,0:T(8,128)(2,1)}) %all-gather.21.cloned.1.call-update) | async-done | bytes 5373968 | tf_op jit(solution)/shard_map/all_gather | solution.py:144
  668.6 7.4 %convert_element_type.742 = f32[512,5248]{1,0:T(8,128)} convert(bf16[512,5248]{1,0:T(8,128)(2,1)} %all-gather.21.cloned.1.call-done) | non-fusion elementwise | flops 2686976 | bytes 16121856 | tf_op jit(solution)/shard_map/convert_element_type | solution.py:145
  (605 shorter events, 395.9 us)
Async XLA Ops:
  7.2 59.7 %all-gather.9.cloned.1.call-start = ((), (), s32[]{:S(2)}) async-start(), calls=%async_computation | async-start | bytes 4718592 | tf_op jit(solution)/shard_map/all_gather | solution.py:72
  9.2 38.3 %collective-permute-start.1 = (bf16[256,3072]{1,0:T(8,128)(2,1)S(1)}, bf16[256,3072]{1,0:T(8,128)(2,1)}, u32[]{:S(2)}, u32[]{:S(2)}) collective-permute-start(bf16[256,3072]{1,0:T(8,128)(2,1)S(1)} %constant_dynamic-slice_fusion.3), channel_id=1, source_target_pairs={{0,1},{1,0},{2,3},{3,2},{4,5},{5,4},{6,7},{7,6},{8,9},{9,8},{10,11... | collective-permute-start | bytes 4718600 | tf_op jit(solution)/shard_map/ppermute | solution.py:62
  12.2 50.3 %collective-permute-start = (f32[2,512]{1,0:T(2,128)S(1)}, f32[2,512]{1,0:T(2,128)S(1)}, u32[]{:S(2)}, u32[]{:S(2)}) collective-permute-start(f32[2,512]{1,0:T(2,128)S(1)} %maximum_convert_fusion), channel_id=1, source_target_pairs={{0,1},{1,0},{2,3},{3,2},{4,5},{5,4},{6,7},{7,6},{8,9},{9,8},{10,11... | collective-permute-start | bytes 12296 | tf_op jit(solution)/shard_map/ppermute | solution.py:62
  13.1 109.7 %collective-permute-start.4 = (bf16[256,1024]{1,0:T(8,128)(2,1)}, bf16[256,1024]{1,0:T(8,128)(2,1)}, u32[]{:S(2)}, u32[]{:S(2)}) collective-permute-start(bf16[256,1024]{1,0:T(8,128)(2,1)} %constant_dynamic-slice_fusion.2), channel_id=1, source_target_pairs={{0,1},{1,0},{2,3},{3,2},{4,5},{5,4},{6,7},{7,6},{8,9},{9,8},{10,11... | collective-permute-start | bytes 1572872 | tf_op jit(solution)/shard_map/ppermute | solution.py:62
  47.5 160.3 %all-gather.11.cloned.1.call-start = ((), (), s32[]{:S(2)}) async-start(), calls=%async_computation.1 | async-start | bytes 1572864 | tf_op jit(solution)/shard_map/all_gather | solution.py:72
  51.0 71.8 %collective-permute-start.5 = (bf16[256,5248]{1,0:T(8,128)(2,1)}, bf16[256,5248]{1,0:T(8,128)(2,1)}, u32[]{:S(2)}, u32[]{:S(2)}) collective-permute-start(bf16[256,5248]{1,0:T(8,128)(2,1)} %constant_dynamic-slice_fusion.1), channel_id=1, source_target_pairs={{0,1},{1,0},{2,3},{3,2},{4,5},{5,4},{6,7},{7,6},{8,9},{9,8},{10,11... | collective-permute-start | bytes 8060936 | tf_op jit(solution)/shard_map/ppermute | solution.py:62
  55.6 88.8 %collective-permute-start.8 = (bf16[656,1024]{1,0:T(8,128)(2,1)}, bf16[656,1024]{1,0:T(8,128)(2,1)}, u32[]{:S(2)}, u32[]{:S(2)}) collective-permute-start(bf16[656,1024]{1,0:T(8,128)(2,1)} %constant_dynamic-slice_fusion), channel_id=1, source_target_pairs={{0,1},{1,0},{2,3},{3,2},{4,5},{5,4},{6,7},{7,6},{8,9},{9,8},{10,11... | collective-permute-start | bytes 4030472 | tf_op jit(solution)/shard_map/ppermute | solution.py:62
  88.3 17.7 %collective-permute-start.3 = (bf16[192,2048]{1,0:T(8,128)(2,1)}, bf16[192,2048]{1,0:T(8,128)(2,1)}, u32[]{:S(2)}, u32[]{:S(2)}) collective-permute-start(bf16[192,2048]{1,0:T(8,128)(2,1)} %pad_maximum_fusion.7), channel_id=1, source_target_pairs={{0,2},{4,0},{8,4},{12,8},{14,12},{10,14},{6,10},{2,6},{1,3},{5,1},... | collective-permute-start | bytes 2359304 | tf_op jit(solution)/shard_map/ppermute | solution.py:58
  122.8 94.6 %all-gather.15.cloned.1.call-start = ((), (), s32[]{:S(2)}) async-start(), calls=%async_computation.3 | async-start | bytes 4030464 | tf_op jit(solution)/shard_map/all_gather | solution.py:72
  144.4 77.0 %all-gather.13.cloned.1.call-start = ((), (), s32[]{:S(2)}) async-start(), calls=%async_computation.2 | async-start | bytes 8060928 | tf_op jit(solution)/shard_map/all_gather | solution.py:72
  148.5 447.1 %all-gather.19.cloned.1.call-start = ((), (), s32[]{:S(2)}) async-start(), calls=%async_computation.5 | async-start | bytes 1114112 | tf_op jit(solution)/shard_map/all_gather | solution.py:144
  148.5 19.0 %collective-permute-start.10 = (bf16[192,2048]{1,0:T(8,128)(2,1)}, bf16[192,2048]{1,0:T(8,128)(2,1)S(1)}, u32[]{:S(2)}, u32[]{:S(2)}) collective-permute-start(bf16[192,2048]{1,0:T(8,128)(2,1)} %collective-permute-done.7), channel_id=1, source_target_pairs={{0,2},{4,0},{8,4},{12,8},{14,12},{10,14},{6,10},{2,6},{1,3},{5,1},... | collective-permute-start | bytes 2359304 | tf_op jit(solution)/shard_map/ppermute | solution.py:58
  150.4 18.3 %collective-permute-start.9 = (bf16[192,2048]{1,0:T(8,128)(2,1)}, bf16[192,2048]{1,0:T(8,128)(2,1)S(1)}, u32[]{:S(2)}, u32[]{:S(2)}) collective-permute-start(bf16[192,2048]{1,0:T(8,128)(2,1)} %collective-permute-done.6), channel_id=1, source_target_pairs={{0,4},{4,8},{8,12},{12,14},{14,10},{10,6},{6,2},{2,0},{1,5},{5,9},... | collective-permute-start | bytes 2359304 | tf_op jit(solution)/shard_map/ppermute | solution.py:58
  173.7 17.5 %collective-permute-start.11 = (bf16[192,2048]{1,0:T(8,128)(2,1)}, bf16[192,2048]{1,0:T(8,128)(2,1)}, u32[]{:S(2)}, u32[]{:S(2)}) collective-permute-start(bf16[192,2048]{1,0:T(8,128)(2,1)} %copy-done.96), channel_id=1, source_target_pairs={{0,4},{4,8},{8,12},{12,14},{14,10},{10,6},{6,2},{2,0},{1,5},{5,9},... | collective-permute-start | bytes 2359304 | tf_op jit(solution)/shard_map/ppermute | solution.py:58
  249.1 33.4 %collective-permute-start.13 = (bf16[2,256,5248]{2,1,0:T(8,128)(2,1)}, bf16[2,256,5248]{2,1,0:T(8,128)(2,1)}, u32[]{:S(2)}, u32[]{:S(2)}) collective-permute-start(bf16[2,256,5248]{2,1,0:T(8,128)(2,1)} %dynamic-slice_bitcast_fusion), channel_id=1, source_target_pairs={{0,16},{16,0},{1,17},{17,1},{2,18},{18,2},{3,19},{19,3},{4,20},{20... | collective-permute-start | bytes 16121864 | tf_op jit(solution)/shard_map/ppermute | solution.py:62
  252.8 25.6 %collective-permute-start.12 = (bf16[2,656,1024]{2,1,0:T(8,128)(2,1)}, bf16[2,656,1024]{2,1,0:T(8,128)(2,1)}, u32[]{:S(2)}, u32[]{:S(2)}) collective-permute-start(bf16[2,656,1024]{2,1,0:T(8,128)(2,1)} %dynamic-slice_bitcast_fusion.3), channel_id=1, source_target_pairs={{0,16},{16,0},{1,17},{17,1},{2,18},{18,2},{3,19},{19,3},{4,20},{20... | collective-permute-start | bytes 8060936 | tf_op jit(solution)/shard_map/ppermute | solution.py:62
  270.3 71.1 %collective-permute-start.17 = (bf16[192,2048]{1,0:T(8,128)(2,1)}, bf16[192,2048]{1,0:T(8,128)(2,1)}, u32[]{:S(2)}, u32[]{:S(2)}) collective-permute-start(bf16[192,2048]{1,0:T(8,128)(2,1)} %copy.156), channel_id=1, source_target_pairs={{0,4},{4,8},{8,12},{12,14},{14,10},{10,6},{6,2},{2,0},{1,5},{5,9},... | collective-permute-start | bytes 2359304 | tf_op jit(solution)/shard_map/ppermute | solution.py:58
  308.8 64.1 %collective-permute-start.15 = (bf16[656,1024]{1,0:T(8,128)(2,1)}, bf16[656,1024]{1,0:T(8,128)(2,1)}, u32[]{:S(2)}, u32[]{:S(2)}) collective-permute-start(bf16[656,1024]{1,0:T(8,128)(2,1)} %dynamic-slice_bitcast_fusion.5), channel_id=1, source_target_pairs={{0,1},{1,0},{2,3},{3,2},{4,5},{5,4},{6,7},{7,6},{8,9},{9,8},{10,11... | collective-permute-start | bytes 4030472 | tf_op jit(solution)/shard_map/ppermute | solution.py:62
  310.9 52.9 %collective-permute-start.16 = (bf16[256,1024]{1,0:T(8,128)(2,1)}, bf16[256,1024]{1,0:T(8,128)(2,1)}, u32[]{:S(2)}, u32[]{:S(2)}) collective-permute-start(bf16[256,1024]{1,0:T(8,128)(2,1)} %dynamic-slice_bitcast_fusion.7), channel_id=1, source_target_pairs={{0,1},{1,0},{2,3},{3,2},{4,5},{5,4},{6,7},{7,6},{8,9},{9,8},{10,11... | collective-permute-start | bytes 1572872 | tf_op jit(solution)/shard_map/ppermute | solution.py:62
  320.7 45.4 %collective-permute-start.21 = (bf16[192,2048]{1,0:T(8,128)(2,1)}, bf16[192,2048]{1,0:T(8,128)(2,1)}, u32[]{:S(2)}, u32[]{:S(2)}) collective-permute-start(bf16[192,2048]{1,0:T(8,128)(2,1)} %copy.161), channel_id=1, source_target_pairs={{0,2},{4,0},{8,4},{12,8},{14,12},{10,14},{6,10},{2,6},{1,3},{5,1},... | collective-permute-start | bytes 2359304 | tf_op jit(solution)/shard_map/ppermute | solution.py:58
  343.7 26.6 %collective-permute-start.18 = (bf16[192,2048]{1,0:T(8,128)(2,1)}, bf16[192,2048]{1,0:T(8,128)(2,1)}, u32[]{:S(2)}, u32[]{:S(2)}) collective-permute-start(bf16[192,2048]{1,0:T(8,128)(2,1)} %add_convert_fusion.5), channel_id=1, source_target_pairs={{0,4},{4,8},{8,12},{12,14},{14,10},{10,6},{6,2},{2,0},{1,5},{5,9},... | collective-permute-start | bytes 2359304 | tf_op jit(solution)/shard_map/ppermute | solution.py:58
  362.3 80.4 %collective-permute-start.25 = (bf16[256,5248]{1,0:T(8,128)(2,1)}, bf16[256,5248]{1,0:T(8,128)(2,1)}, u32[]{:S(2)}, u32[]{:S(2)}) collective-permute-start(bf16[256,5248]{1,0:T(8,128)(2,1)} %dynamic-slice_bitcast_fusion.2), channel_id=1, source_target_pairs={{0,1},{1,0},{2,3},{3,2},{4,5},{5,4},{6,7},{7,6},{8,9},{9,8},{10,11... | collective-permute-start | bytes 8060936 | tf_op jit(solution)/shard_map/ppermute | solution.py:62
  368.7 18.5 %collective-permute-start.22 = (bf16[192,2048]{1,0:T(8,128)(2,1)}, bf16[192,2048]{1,0:T(8,128)(2,1)}, u32[]{:S(2)}, u32[]{:S(2)}) collective-permute-start(bf16[192,2048]{1,0:T(8,128)(2,1)} %add_convert_fusion.2), channel_id=1, source_target_pairs={{0,2},{4,0},{8,4},{12,8},{14,12},{10,14},{6,10},{2,6},{1,3},{5,1},... | collective-permute-start | bytes 2359304 | tf_op jit(solution)/shard_map/ppermute | solution.py:58
  372.6 18.2 %collective-permute-start.19 = (bf16[192,2048]{1,0:T(8,128)(2,1)}, bf16[192,2048]{1,0:T(8,128)(2,1)}, u32[]{:S(2)}, u32[]{:S(2)}) collective-permute-start(bf16[192,2048]{1,0:T(8,128)(2,1)} %add_convert_fusion.4), channel_id=1, source_target_pairs={{0,4},{4,8},{8,12},{12,14},{14,10},{10,6},{6,2},{2,0},{1,5},{5,9},... | collective-permute-start | bytes 2359304 | tf_op jit(solution)/shard_map/ppermute | solution.py:58
  436.9 19.0 %collective-permute-start.38 = (bf16[32,1024]{1,0:T(8,128)(2,1)}, bf16[32,1024]{1,0:T(8,128)(2,1)S(1)}, u32[]{:S(2)}, u32[]{:S(2)}) collective-permute-start(bf16[32,1024]{1,0:T(8,128)(2,1)} %get-tuple-element.111), channel_id=1, source_target_pairs={{0,2},{4,0},{8,4},{12,8},{14,12},{10,14},{6,10},{2,6},{1,3},{5,1},... | collective-permute-start | bytes 196616 | tf_op jit(solution)/shard_map/ppermute | solution.py:58
  451.6 37.4 %collective-permute-start.26 = (bf16[256,3200]{1,0:T(8,128)(2,1)}, bf16[256,3200]{1,0:T(8,128)(2,1)}, u32[]{:S(2)}, u32[]{:S(2)}) collective-permute-start(bf16[256,3200]{1,0:T(8,128)(2,1)} %dynamic-slice_bitcast_fusion.4), channel_id=1, source_target_pairs={{0,1},{1,0},{2,3},{3,2},{4,5},{5,4},{6,7},{7,6},{8,9},{9,8},{10,11... | collective-permute-start | bytes 4915208 | tf_op jit(solution)/shard_map/ppermute | solution.py:62
  467.9 130.5 %all-gather.23.cloned.1.call-start = ((), (), s32[]{:S(2)}) async-start(), calls=%async_computation.7 | async-start | bytes 2854912 | tf_op jit(solution)/shard_map/all_gather | solution.py:144
  473.9 18.6 %collective-permute-start.53 = (bf16[656,128]{1,0:T(8,128)(2,1)S(1)}, bf16[656,128]{1,0:T(8,128)(2,1)S(1)}, u32[]{:S(2)}, u32[]{:S(2)}) collective-permute-start(bf16[656,128]{1,0:T(8,128)(2,1)S(1)} %get-tuple-element.97), channel_id=1, source_target_pairs={{0,2},{4,0},{8,4},{12,8},{14,12},{10,14},{6,10},{2,6},{1,3},{5,1},... | collective-permute-start | bytes 503816 | tf_op jit(solution)/shard_map/ppermute | solution.py:58
  475.6 26.1 %collective-permute-start.51 = (bf16[656,128]{1,0:T(8,128)(2,1)S(1)}, bf16[656,128]{1,0:T(8,128)(2,1)S(1)}, u32[]{:S(2)}, u32[]{:S(2)}) collective-permute-start(bf16[656,128]{1,0:T(8,128)(2,1)S(1)} %get-tuple-element.96), channel_id=1, source_target_pairs={{0,4},{4,8},{8,12},{12,14},{14,10},{10,6},{6,2},{2,0},{1,5},{5,9},... | collective-permute-start | bytes 503816 | tf_op jit(solution)/shard_map/ppermute | solution.py:58
  503.3 106.9 %all-gather.17.cloned.1.call-start = ((), (), s32[]{:S(2)}) async-start(), calls=%async_computation.4 | async-start | bytes 3481600 | tf_op jit(solution)/shard_map/all_gather | solution.py:144
  519.6 34.7 %collective-permute-start.45 = (bf16[32,5248]{1,0:T(8,128)(2,1)}, bf16[32,5248]{1,0:T(8,128)(2,1)}, u32[]{:S(2)}, u32[]{:S(2)}) collective-permute-start(bf16[32,5248]{1,0:T(8,128)(2,1)} %get-tuple-element.89), channel_id=1, source_target_pairs={{0,2},{4,0},{8,4},{12,8},{14,12},{10,14},{6,10},{2,6},{1,3},{5,1},... | collective-permute-start | bytes 1007624 | tf_op jit(solution)/shard_map/ppermute | solution.py:58
  538.5 130.1 %all-gather.21.cloned.1.call-start = ((), (), s32[]{:S(2)}) async-start(), calls=%async_computation.6 | async-start | bytes 5709824 | tf_op jit(solution)/shard_map/all_gather | solution.py:144
  (174 other events, 893.6 us)
Sparse Core Ops, SparseCore 0:
  47.6 13.9 all-gather.8
  122.9 9.3 all-gather.10
  144.5 12.9 all-gather.14
  158.9 16.5 all-gather.12
  468.0 40.2 all-gather.18
  510.4 47.9 all-gather.22
  561.2 48.9 all-gather.16
  613.0 55.5 all-gather.20
